TPU v7x, 256 devices: a whole 4x4x8 slice. The times are simulated.
256 devices in a mesh: ctx: 32 (over y, z), head: 8 (over x, core).
Axes of the slice: x: 4, y: 4, z: 8, core: 2. Of those that a mesh axis runs over, the one named last changes fastest.
Arguments:
- qkv_tiles: bfloat16 [12288, 3, 3072], P('ctx', None, 'head'), may hold values from -100 to 100
- seq_pos: int32 [12288], P('ctx'), may hold values from 0 to 12287, as said below
- rope_pos: int32 [3, 12288], P(None, 'ctx'), may hold values from 0 to 79
- text_keys: bfloat16 [256, 3072], P('ctx', 'head'), may hold values from -100 to 100
- text_values: bfloat16 [256, 3072], P('ctx', 'head'), may hold values from -48 to 48
- text_len: int32 [1], replicated, may hold values from 32 to 256
- q_gain: float32 [128], replicated, may hold values from 0.8 to 1.7
- k_gain: float32 [128], replicated, may hold values from 0.8 to 1.7
- w_out: bfloat16 [3072, 3072], P('head'), may hold values from -0.75 to 0.75
- b_out: float32 [3072], P('head'), may hold values from -3 to 3
Outputs:
- mixed: bfloat16 [12288, 3072], P('ctx', 'head')
Inputs may be any that keep to these rules, and one draw needn't show every extreme that they name: `seq_pos`: a permutation of the sequence positions; every owner sends to every context shard between 6 and 24 rows, exactly 24 to some shard; the multiset of these counts is the same for every owner and every shard; the rows one owner sends to one shard take a contiguous run of that shard's positions.
All inputs are finite; a program needn't handle non-finite values.
Results may differ from a plain program's by a relative error of at most 0.019.
Values may be sent and summed in bfloat16 or wider, within the bound.
A program may use at most 64 MiB of HBM per device.

v0:
```python
import jax
import jax.numpy as jnp
from jax import lax
from jax.sharding import PartitionSpec as P

HD = 128
WINDOW = 3


def shifted(block, axis, distance):
    devices = range(lax.axis_size(axis))
    route = [(i - distance, i) for i in devices if i - distance in devices]
    return lax.ppermute(block, axis, route)


def rms_scale(x, gain_vec):
    return x * lax.rsqrt(jnp.mean(x * x, axis=-1, keepdims=True) + 1e-06) * gain_vec


def rope_tables(positions, head_dim):
    seg_time = head_dim // 8
    seg_space = (head_dim - seg_time) // 2
    tables = []
    for axis_index, seg_width in ((0, seg_time), (1, seg_space), (2, seg_space)):
        frequency = 256.0 ** (-jnp.arange(0, seg_width, 2, dtype=jnp.float32) / seg_width)
        angles = positions[axis_index].astype(jnp.float32)[:, None] * frequency[None, :]
        tables.append((jnp.cos(angles), jnp.sin(angles), seg_width))
    return tables


def rotate(x, tables):
    pieces = []
    offset = 0
    for cos_part, sin_part, seg_width in tables:
        half_width = seg_width // 2
        lower_part = x[..., offset : offset + half_width]
        upper_part = x[..., offset + half_width : offset + seg_width]
        cos_b = cos_part[:, None, :]
        sin_b = sin_part[:, None, :]
        pieces.append(lower_part * cos_b - upper_part * sin_b)
        pieces.append(upper_part * cos_b + lower_part * sin_b)
        offset += seg_width
    return jnp.concatenate(pieces, axis=-1)


def key_normed(tile_rows, k_gain):
    head_count = tile_rows.shape[2] // HD
    return rms_scale(
        tile_rows[:, 1].astype(jnp.float32).reshape(tile_rows.shape[0], head_count, HD), k_gain
    )


def attend_block(query_b, kv_block, live_mask, running):
    numerator, denominator = running
    scores = jnp.einsum(
        "qhd,khd->hqk", query_b, kv_block[0], preferred_element_type=jnp.float32
    ) * HD ** (-0.5)
    weights = jnp.where(live_mask, jnp.exp(scores), 0.0)
    denominator = denominator + jnp.sum(weights, axis=-1)
    numerator = numerator + jnp.einsum(
        "hqk,khd->qhd",
        weights.astype(jnp.bfloat16),
        kv_block[1],
        preferred_element_type=jnp.float32,
    )
    return (numerator, denominator)


def on_device(
    qkv_tiles, seq_pos, rope_pos, text_keys, text_values, text_len, q_gain, k_gain, w_out, b_out
):
    row_count = qkv_tiles.shape[0]
    span_width = qkv_tiles.shape[2]
    head_count = span_width // HD
    shards = lax.axis_size("ctx")
    capacity = 2 * row_count // shards
    target = seq_pos // row_count
    onehot = (target[:, None] == jnp.arange(shards, dtype=jnp.int32)[None, :]).astype(jnp.int32)
    before = jnp.cumsum(onehot, axis=0) - onehot
    slot_rank = jnp.sum(before * onehot, axis=1)
    slot_index = target * capacity + slot_rank
    outgoing = (
        jnp.zeros((shards * capacity, 3, span_width), jnp.bfloat16).at[slot_index].set(qkv_tiles)
    )
    places = (
        jnp.full((shards * capacity,), row_count, jnp.int32).at[slot_index].set(seq_pos % row_count)
    )
    incoming, incoming_places = (
        lax.all_to_all(
            outgoing.reshape(shards, capacity, 3, span_width),
            "ctx",
            split_axis=0,
            concat_axis=0,
            tiled=True,
        ),
        lax.all_to_all(
            places.reshape(shards, capacity), "ctx", split_axis=0, concat_axis=0, tiled=True
        ),
    )
    routed = (
        jnp.zeros((row_count, 3, span_width), jnp.bfloat16)
        .at[incoming_places.reshape(-1)]
        .set(incoming.reshape(shards * capacity, 3, span_width), mode="drop")
    )
    key_n = key_normed(routed, k_gain)
    partial_value = jnp.sum(key_n, axis=0)
    key_mean = lax.psum(partial_value, "ctx") / (row_count * shards)
    query_n = rms_scale(routed[:, 0].astype(jnp.float32).reshape(row_count, head_count, HD), q_gain)
    tables = rope_tables(rope_pos, HD)
    query_b = rotate(query_n, tables).astype(jnp.bfloat16)
    key_b = rotate(key_n - key_mean, tables).astype(jnp.bfloat16)
    value_b = routed[:, 2].reshape(row_count, head_count, HD)
    own_block = jnp.stack([key_b, value_b])
    text_k, text_v = (
        lax.all_gather(text_keys, "ctx", axis=0, tiled=True),
        lax.all_gather(text_values, "ctx", axis=0, tiled=True),
    )
    text_count = text_k.shape[0]
    text_kb = (
        rms_scale(text_k.astype(jnp.float32).reshape(text_count, head_count, HD), k_gain) - key_mean
    ).astype(jnp.bfloat16)
    text_block = jnp.stack([text_kb, text_v.reshape(text_count, head_count, HD)])
    text_live = (jnp.arange(text_count, dtype=jnp.int32) < text_len[0])[None, None, :]
    running = (
        jnp.zeros((row_count, head_count, HD), jnp.float32),
        jnp.zeros((head_count, row_count), jnp.float32),
    )
    running = attend_block(query_b, own_block, True, running)
    running = attend_block(query_b, text_block, text_live, running)
    my_index = lax.axis_index("ctx")
    moving = own_block
    for distance in range(1, WINDOW + 1):
        moving = shifted(moving, "ctx", 1)
        running = attend_block(query_b, moving, my_index >= distance, running)
    numerator, denominator = running
    attended = (
        (numerator / denominator.T[:, :, None]).astype(jnp.bfloat16).reshape(row_count, span_width)
    )
    summed = lax.psum_scatter(
        lax.dot_general(
            w_out, attended, (((0,), (1,)), ((), ())), preferred_element_type=jnp.float32
        ).astype(jnp.bfloat16),
        "head",
        scatter_dimension=0,
        tiled=True,
    ).astype(jnp.float32)
    return (summed + b_out[:, None]).T.astype(jnp.bfloat16)


def solution(mesh):
    in_specs = (
        P("ctx", None, "head"),
        P("ctx"),
        P(None, "ctx"),
        P("ctx", "head"),
        P("ctx", "head"),
        P(),
        P(),
        P(),
        P("head", None),
        P("head"),
    )
    out_specs = P("ctx", "head")
    return jax.shard_map(
        on_device, mesh=mesh, in_specs=in_specs, out_specs=out_specs, check_vma=False
    )
```

profile of v0, /device:TPU:1, one launch (start us, length us, event | category | flops | bytes accessed | tf_op | source)
XLA Modules:
  0.0 460.9 jit_solution(7359209933007351804)
XLA Ops:
  6.5 0.8 add_select_fusion
  7.4 0.9 reduce-window.6
  8.7 2.9 scatter_custom_fusion
  12.3 12.0 %all-to-all-start = ((s32[32,1,24]{2,1,0:T(1,128)}), s32[32,1,24]{2,1,0:T(1,128)S(1)}, u32[]{:S(2)}, u32[]{:S(2)}) async-start(s32[32,1,24]{2,1,0:T(1,128)} %bitcast.2), calls=%async_computation | async-start | bytes 32768 | tf_op jit(solution)/shard_map/all_to_all | solution.py:96
  24.3 1.9 copy.74
  26.3 2.1 broadcast_in_dim.22
  28.3 42.3 %scatter_fusion = bf16[768,3,384]{2,1,0:T(4,128)(2,1)} fusion(bf16[768,3,384]{2,1,0:T(4,128)(2,1)} %broadcast_in_dim.22, s32[384]{0:T(512)} %copy-done.16, bf16[384,3,384]{2,1,0:T(4,128)(2,1)S(1)} %copy.74), kind=kCustom, calls=%fused_computation.1 | custom fusion | bytes 2655744 | tf_op jit(solution)/shard_map/scatter | solution.py:83
  70.6 3.1 copy.76
  73.8 9.5 %all-to-all-start.1 = ((bf16[32,24,3,384]{3,1,2,0:T(8,128)(2,1)}), bf16[32,24,3,384]{3,1,2,0:T(8,128)(2,1)}, u32[]{:S(2)}, u32[]{:S(2)}) async-start(bf16[32,24,3,384]{3,1,2,0:T(8,128)(2,1)} %copy.76), calls=%async_computation.1 | async-start | bytes 3538944 | tf_op jit(solution)/shard_map/all_to_all | solution.py:89
  83.5 0.8 copy.84
  85.1 68.1 %all_gather.7 = bf16[256,384]{1,0:T(8,128)(2,1)S(1)} all-gather(bf16[8,384]{1,0:T(8,128)(2,1)S(1)} %copy-done.18), channel_id=1, replica_groups=mesh['ctx'=32,'head'=8] {'ctx'}, dimensions={0}, use_global_device_ids=true | all-gather | bytes 202752 | tf_op jit(solution)/shard_map/all_gather | solution.py:116
  154.0 35.2 %all_gather.6 = bf16[256,384]{1,0:T(8,128)(2,1)S(1)} all-gather(bf16[8,384]{1,0:T(8,128)(2,1)S(1)} %copy-done.19), channel_id=1, replica_groups=mesh['ctx'=32,'head'=8] {'ctx'}, dimensions={0}, use_global_device_ids=true | all-gather | bytes 202752 | tf_op jit(solution)/shard_map/all_gather | solution.py:115
  191.9 2.4 multiply_cosine_fusion
  195.6 1.7 copy.77
  197.3 2.9 copy.78
  200.5 59.0 %scatter_fusion.1 = bf16[384,3,384]{2,1,0:T(4,128)(2,1)S(1)} fusion(bf16[384,3,384]{2,1,0:T(4,128)(2,1)S(1)} %broadcast_in_dim.20, s32[768]{0:T(1024)S(1)} %fusion.30, bf16[768,3,384]{2,1,0:T(4,128)(2,1)} %copy.78), kind=kCustom, calls=%fused_computation.2 | custom fusion | bytes 5311488 | tf_op jit(solution)/shard_map/scatter | solution.py:103
  259.6 2.3 fusion.35
  261.8 0.8 copy-done.1
  262.7 0.9 copy_convert_fusion
  263.5 1.4 copy.86
  264.9 1.1 copy.87
  266.3 1.1 copy.82
  267.5 2.2 copy.79
  269.7 0.9 mul.376.clone
  270.5 2.1 copy.89
  272.7 1.2 multiply_reduce_fusion
  273.9 57.9 %psum.7 = f32[3,128]{1,0:T(4,128)S(1)} all-reduce(f32[3,128]{1,0:T(4,128)S(1)} %bitcast.131), channel_id=1, replica_groups=mesh['ctx'=32,'head'=8] {'ctx'}, use_global_device_ids=true, to_apply=%region_9.10 | all-reduce | flops 384 | bytes 3072 | tf_op jit(solution)/shard_map/psum | solution.py:107
  331.8 0.9 copy.96
  332.6 1.3 multiply_subtract_fusion
  333.9 1.3 multiply_multiply_fusion
  335.3 2.5 add_convert_fusion.3
  337.8 1.5 add_convert_fusion.1
  339.3 2.4 concatenate.38
  341.7 1.9 pad_maximum_fusion
  343.7 2.2 collective-permute-start
  345.8 2.9 add_convert_fusion.4
  348.7 2.5 concatenate.31
  351.2 1.9 concatenate.30
  354.1 2.1 collective-permute-start.1
  357.1 1.5 fusion.38
  358.6 4.6 collective-permute-done.1
  363.1 3.7 collective-permute-start.2
  366.9 1.4 fusion.9
  369.2 4.4 collective-permute-done.2
  374.6 2.8 fusion
  377.4 4.3 copy.114
  381.7 70.4 %reduce-scatter.4.cloned.1.call-done = bf16[384,384]{1,0:T(8,128)(2,1)} async-done(((bf16[3072,384]{1,0:T(8,128)(2,1)}), bf16[384,384]{1,0:T(8,128)(2,1)}) %reduce-scatter.4.cloned.1.call-update) | async-done | bytes 294928
  452.2 1.2 copy.115
  (97 shorter events, 11.3 us)
Async XLA Ops:
  6.5 368.1 %copy-start = (bf16[384,3072]{1,0:T(8,128)(2,1)S(1)}, bf16[384,3072]{1,0:T(8,128)(2,1)}, u32[]{:S(2)}) copy-start(bf16[384,3072]{1,0:T(8,128)(2,1)} %param.18) | copy-start | bytes 7077892
  8.7 3.6 copy-start.16
  12.3 61.5 %all-to-all-start = ((s32[32,1,24]{2,1,0:T(1,128)}), s32[32,1,24]{2,1,0:T(1,128)S(1)}, u32[]{:S(2)}, u32[]{:S(2)}) async-start(s32[32,1,24]{2,1,0:T(1,128)} %bitcast.2), calls=%async_computation | async-start | bytes 32768 | tf_op jit(solution)/shard_map/all_to_all | solution.py:96
  73.8 9.6 %copy-start.21 = (s32[3,384]{1,0:T(4,128)S(1)}, s32[3,384]{1,0:T(4,128)}, u32[]{:S(2)}) copy-start(s32[3,384]{1,0:T(4,128)} %param.12) | copy-start | bytes 13828
  73.8 11.4 %copy-start.18 = (bf16[8,384]{1,0:T(8,128)(2,1)S(1)}, bf16[8,384]{1,0:T(8,128)(2,1)}, u32[]{:S(2)}) copy-start(bf16[8,384]{1,0:T(8,128)(2,1)} %param.14) | copy-start | bytes 18436
  73.8 80.3 %copy-start.19 = (bf16[8,384]{1,0:T(8,128)(2,1)S(1)}, bf16[8,384]{1,0:T(8,128)(2,1)}, u32[]{:S(2)}) copy-start(bf16[8,384]{1,0:T(8,128)(2,1)} %param.13) | copy-start | bytes 18436
  73.8 121.9 %all-to-all-start.1 = ((bf16[32,24,3,384]{3,1,2,0:T(8,128)(2,1)}), bf16[32,24,3,384]{3,1,2,0:T(8,128)(2,1)}, u32[]{:S(2)}, u32[]{:S(2)}) async-start(bf16[32,24,3,384]{3,1,2,0:T(8,128)(2,1)} %copy.76), calls=%async_computation.1 | async-start | bytes 3538944 | tf_op jit(solution)/shard_map/all_to_all | solution.py:89
  83.3 107.5 %copy-start.23 = (f32[128]{0:T(128)S(1)}, f32[128]{0:T(128)}, u32[]{:S(2)}) copy-start(f32[128]{0:T(128)} %param.17) | copy-start | bytes 1540
  83.3 368.9 %reduce-scatter.4.cloned.1.call-start = ((), (), s32[]{:S(2)}) async-start(), calls=%async_computation.3 | async-start | bytes 2654208
  189.4 7.9 %copy-start.12 = (bf16[256,384]{0,1:T(8,128)(2,1)}, bf16[256,384]{0,1:T(8,128)(2,1)S(1)}, u32[]{:S(2)}) copy-start(bf16[256,384]{0,1:T(8,128)(2,1)S(1)} %copy.91) | copy-start | bytes 589828
  261.8 0.8 copy-start.1
  263.5 2.5 copy-start.5
  267.4 5.3 %copy-start.2 = (bf16[384,1,384]{2,1,0:T(2,128)(2,1)S(1)}, bf16[384,1,384]{2,1,0:T(2,128)(2,1)}, u32[]{:S(2)}) copy-start(bf16[384,1,384]{2,1,0:T(2,128)(2,1)} %copy-done.1) | copy-start | bytes 884740
  267.4 5.2 %copy-start.17 = (f32[384]{0:T(512)S(1)}, f32[384]{0:T(512)}, u32[]{:S(2)}) copy-start(f32[384]{0:T(512)} %broadcast_bitcast_fusion) | copy-start | bytes 4612
  269.7 63.0 %copy-start.3 = (bf16[384,1,384]{0,2,1:T(8,128)(2,1)}, bf16[384,1,384]{0,2,1:T(8,128)(2,1)S(1)}, u32[]{:S(2)}) copy-start(bf16[384,1,384]{0,2,1:T(8,128)(2,1)S(1)} %copy.79) | copy-start | bytes 884740
  269.7 63.0 %copy-start.24 = (f32[128]{0:T(128)S(1)}, f32[128]{0:T(128)}, u32[]{:S(2)}) copy-start(f32[128]{0:T(128)} %param.17) | copy-start | bytes 1540
  272.7 61.3 %copy-start.25 = (f32[128]{0:T(128)S(1)}, f32[128]{0:T(128)}, u32[]{:S(2)}) copy-start(f32[128]{0:T(128)} %param.16) | copy-start | bytes 1540
  273.9 61.4 %copy-start.15 = (f32[384,8]{1,0:T(8,128)S(1)}, f32[384,8]{1,0:T(8,128)}, u32[]{:S(2)}) copy-start(f32[384,8]{1,0:T(8,128)} %copy.84) | copy-start | bytes 36868
  335.2 2.5 copy-start.6
  335.2 2.5 copy-start.7
  335.3 2.5 copy-start.8
  335.3 2.5 copy-start.9
  343.7 10.4 %collective-permute-start = (bf16[2,384,3,128]{3,1,2,0:T(8,128)(2,1)}, bf16[2,384,3,128]{3,1,2,0:T(8,128)(2,1)}, u32[]{:S(2)}, u32[]{:S(2)}) collective-permute-start(bf16[2,384,3,128]{3,1,2,0:T(8,128)(2,1)} %pad_maximum_fusion), channel_id=1, source_target_pairs={{0,8},{8,16},{16,24},{24,32},{32,40},{40,48},{48,56},{56,64},{64,7... | collective-permute-start | bytes 1769480 | tf_op jit(solution)/shard_map/ppermute | solution.py:13
  348.7 2.5 copy-start.10
  351.2 2.0 copy-start.11
  351.2 2.4 copy-start.4
  353.6 2.6 copy-start.13
  353.6 2.6 copy-start.20
  353.6 2.6 copy-start.26
  353.6 3.2 copy-start.14
  354.1 9.0 %collective-permute-start.1 = (bf16[2,384,3,128]{3,1,2,0:T(8,128)(2,1)}, bf16[2,384,3,128]{3,1,2,0:T(8,128)(2,1)S(1)}, u32[]{:S(2)}, u32[]{:S(2)}) collective-permute-start(bf16[2,384,3,128]{3,1,2,0:T(8,128)(2,1)} %collective-permute-done), channel_id=1, source_target_pairs={{0,8},{8,16},{16,24},{24,32},{32,40},{40,48},{48,56},{56,64},{64,7... | collective-permute-start | bytes 1769480 | tf_op jit(solution)/shard_map/ppermute | solution.py:13
  363.1 10.5 %collective-permute-start.2 = (bf16[2,384,3,128]{3,1,2,0:T(8,128)(2,1)S(1)}, bf16[2,384,3,128]{3,1,2,0:T(8,128)(2,1)S(1)}, u32[]{:S(2)}, u32[]{:S(2)}) collective-permute-start(bf16[2,384,3,128]{3,1,2,0:T(8,128)(2,1)S(1)} %collective-permute-done.1), channel_id=1, source_target_pairs={{0,8},{8,16},{16,24},{24,32},{32,40},{40,48},{48,56},{56,64},{64,7... | collective-permute-start | bytes 1769480 | tf_op jit(solution)/shard_map/ppermute | solution.py:13
  381.7 71.6 %copy-start.22 = (f32[384]{0:T(512)S(1)}, f32[384]{0:T(512)}, u32[]{:S(2)}) copy-start(f32[384]{0:T(512)} %param.19) | copy-start | bytes 4612
Sparse Core Ops, SparseCore 0:
  381.9 70.2 reduce-scatter.3
where the time goes:
time: 467 us; the launch traced here: 461 us
  blocking collectives  161 us (34%)
  local copies, waits for them, and re-layouts  146 us (31%)
  waiting for transfers between devices  79.4 us (17%)
  starting transfers between devices  29.6 us (6%)
  other arithmetic  20.8 us (4%)
  between operations  14.6 us (3%)
  matrix products  9.24 us (2%)
    unnamed x2, waiting for transfers between devices  70.4 us
    all_gather x1, blocking collectives, on_device(): lax.all_gather(text_values, 'ctx', axis=0, tiled=True)  68.1 us
    scatter x1, local copies, waits for them, and re-layouts, on_device(): routed = jnp.zeros((row_count, 3, span_width), jnp.bfloat16).at[incoming_...  59 us
    psum x1, blocking collectives, on_device(): key_mean = lax.psum(partial_value, 'ctx') / (row_count * shards)  57.9 us
    scatter x1, local copies, waits for them, and re-layouts, on_device(): jnp.zeros((shards * capacity, 3, span_width), jnp.bfloat16).at[slot_index]  42.3 us
    all_gather x1, blocking collectives, on_device(): lax.all_gather(text_keys, 'ctx', axis=0, tiled=True)  35.2 us
    all_to_all x1, starting transfers between devices, on_device(): lax.all_to_all(places.reshape(shards, capacity), 'ctx', split_axis=0, con...  12 us
    all_to_all x1, starting transfers between devices, on_device(): lax.all_to_all(outgoing.reshape(shards, capacity, 3, span_width), 'ctx',...  9.48 us
  transfers between devices with their start and end apart: 6, of which 3 were waited for; matrix products, arithmetic and copies ran while one was open for 15% of the time, Pallas kernels for 0%

commit v1 on v0

v1 whole, which is shorter than its diff:
```python
import functools

import jax
import jax.numpy as jnp
import numpy as np
from jax import lax
from jax.experimental import pallas as pl
from jax.experimental.pallas import tpu as pltpu
from jax.sharding import PartitionSpec as P

MESH = pl.DeviceIdType.MESH
BF = jnp.bfloat16
F32 = jnp.float32
NC = 32
NY, NZ = 4, 8
NH = 8
T = 384
HL = 3
HD = 128
CAP = 24
CUT = 16
ROWS = 9 * 16 + 5 * 16
WINDOW = 3
TXT = 256
TXD = 8
SCALE = float(np.log2(np.e) / np.sqrt(HD))


def iota(shape, axis):
    return lax.broadcasted_iota(jnp.int32, shape, axis)


def onehot(mask):
    return jnp.where(mask, 1.0, 0.0).astype(BF)


def dot(a, b, ca=1, cb=0):
    return lax.dot_general(a, b, (((ca,), (cb,)), ((), ())), preferred_element_type=F32)


def partner_of(lane):
    up = (lane < 8) | ((lane >= 16) & (lane < 44)) | ((lane >= 72) & (lane < 100))
    half = jnp.where(lane < 16, 8, 28)
    return jnp.where(up, lane + half, lane - half), up


def partner_rows(v):
    lane = iota(v.shape, 1)
    _, up = partner_of(lane)
    near = jnp.where(up, pltpu.roll(v, HD - 8, 1), pltpu.roll(v, 8, 1))
    far = jnp.where(up, pltpu.roll(v, HD - 28, 1), pltpu.roll(v, 28, 1))
    return jnp.where(lane < 16, near, far)


def rms_factor(x):
    return lax.rsqrt(jnp.mean(x * x, axis=-1, keepdims=True) + 1e-06)


def greet(peers):
    barrier = pltpu.get_barrier_semaphore()
    for peer in peers:
        pl.semaphore_signal(barrier, inc=1, device_id=peer, device_id_type=MESH)


def met(count):
    pl.semaphore_wait(pltpu.get_barrier_semaphore(), count)


def route_kernel(
    x_ref, pos_ref, rope_ref, tk_ref, tv_ref, qg_ref, kg_ref, freq_ref, w_ref,
    q_out, kv_out, t_out, wf_out,
    send, recv, tbuf, tab, ssem, rsem, tzs, tzr, tys, tyr, wss, wrs, lsem,
):
    me = lax.axis_index("ctx")
    hd = lax.axis_index("head")
    my, mz = me // NZ, me % NZ

    def signal_ctx(d, c):
        pl.semaphore_signal(
            pltpu.get_barrier_semaphore(), inc=1,
            device_id=((me + d) % NC, hd), device_id_type=MESH,
        )
        return c

    lax.fori_loop(1, NC, signal_ctx, 0)
    greet([(me, (hd + d) % NH) for d in range(1, NH)])

    pos = pos_ref[...]
    shard = ((pos >> 7) * 171) >> 9
    mine = iota((NC, T), 0) == shard
    first = jnp.min(jnp.where(mine, pos, 1 << 20), axis=1, keepdims=True)
    count = jnp.sum(jnp.where(mine, 1, 0), axis=1, keepdims=True)
    rank = pos - jnp.sum(jnp.where(mine, first, 0), axis=0, keepdims=True)
    code_a = jnp.where(rank < CUT, shard * 16 + rank, -100)
    code_b = jnp.where(rank < CUT, -100, shard * 16 + rank - CUT)
    slot = iota((NC * 16, T), 0)
    pick_a = onehot(slot == code_a)
    pick_b = onehot((slot == code_b) | (slot == code_b + 8))

    kg = kg_ref[...]
    sub16 = iota((16, HD), 0)
    extra = jnp.zeros((16, HD), F32)
    for h in range(HL):
        k = x_ref[1, :, h * HD:(h + 1) * HD].astype(F32)
        total = jnp.sum(k * rms_factor(k), axis=0, keepdims=True) * kg
        high = total.astype(BF).astype(F32)
        extra = jnp.where(sub16 == 9 + h, high, extra)
        extra = jnp.where(sub16 == 12 + h, total - high, extra)
    start = first - iota((NC, 1), 0) * T
    lane = iota((NC, HD), 1)
    meta = jnp.where(lane < 32, start >> 4, jnp.where(lane < 64, start & 15, count)).astype(F32)
    row3 = iota((NC, 16, HD), 1)
    extra = jnp.where(row3 == 8, meta[:, None, :], extra[None])

    for c in range(9):
        block = x_ref[c // 3, :, (c % 3) * HD:(c % 3 + 1) * HD]
        send[:, c * 16:(c + 1) * 16, :] = dot(pick_a, block).astype(BF).reshape(NC, 16, HD)
        late = dot(pick_b, block).reshape(NC, 16, HD)
        if c % 2 == 0:
            even = late
        else:
            base = 144 + (c // 2) * 16
            send[:, base:base + 16, :] = jnp.where(row3 < 8, even, late).astype(BF)
    send[:, 208:224, :] = jnp.where(row3 < 8, even, extra).astype(BF)
    tbuf[my, mz] = jnp.concatenate(
        [tk_ref[...].astype(F32), tv_ref[...].astype(F32)], axis=0
    ).astype(BF)
    recv[me] = send[me]

    met(NC - 1 + NH - 1)

    def text_z(d):
        z = (mz + d) % NZ
        return pltpu.make_async_remote_copy(
            src_ref=tbuf.at[my, mz], dst_ref=tbuf.at[my, mz], send_sem=tzs.at[d], recv_sem=tzr.at[d],
            device_id=(my * NZ + z, hd), device_id_type=MESH,
        )

    def text_y(d):
        y = (my + d) % NY
        return pltpu.make_async_remote_copy(
            src_ref=tbuf.at[my], dst_ref=tbuf.at[my], send_sem=tys.at[d], recv_sem=tyr.at[d],
            device_id=(y * NZ + mz, hd), device_id_type=MESH,
        )

    def piece(d):
        to = (me + d) % NC
        return pltpu.make_async_remote_copy(
            src_ref=send.at[to], dst_ref=recv.at[me], send_sem=ssem.at[d], recv_sem=rsem.at[d],
            device_id=(to, hd), device_id_type=MESH,
        )

    def weight(d):
        to = (hd + d) % NH
        return pltpu.make_async_remote_copy(
            src_ref=w_ref.at[:, :, pl.ds(pl.multiple_of(to * T, T), T)],
            dst_ref=wf_out.at[:, pl.ds(pl.multiple_of(hd * HD, HD), HD), :],
            send_sem=wss.at[d], recv_sem=wrs.at[d],
            device_id=(me, to), device_id_type=MESH,
        )

    def start_of(make):
        def go(d, c):
            make(d).start()
            return c
        return go

    def landed(make):
        def go(d, c):
            make(d).wait_recv()
            return c
        return go

    def left(make):
        def go(d, c):
            make(d).wait_send()
            return c
        return go

    lax.fori_loop(1, NZ, start_of(text_z), 0)
    lax.fori_loop(1, NC, start_of(piece), 0)
    lax.fori_loop(1, NH, start_of(weight), 0)
    own_w = pltpu.make_async_copy(
        w_ref.at[:, :, pl.ds(pl.multiple_of(hd * T, T), T)],
        wf_out.at[:, pl.ds(pl.multiple_of(hd * HD, HD), HD), :], lsem,
    )
    own_w.start()

    lane_t = iota((T, HD), 1)
    _, up = partner_of(lane_t)
    eye = iota((T, T), 0) == iota((T, T), 1)
    col = []
    for a in range(3):
        row = rope_ref[a:a + 1, :].astype(F32)
        col.append(jnp.sum(jnp.where(eye, row, 0.0), axis=1, keepdims=True))
    at = jnp.where(lane_t < 16, col[0], jnp.where(lane_t < 72, col[1], col[2]))
    angle = at * freq_ref[...]
    tab[0] = jnp.cos(angle)
    sine = jnp.sin(angle)
    tab[1] = jnp.where(up, -sine, sine)

    lax.fori_loop(1, NZ, landed(text_z), 0)
    lax.fori_loop(1, NY, start_of(text_y), 0)
    lax.fori_loop(1, NC, landed(piece), 0)

    tail = recv[:, 208:224, :].astype(F32)
    sums = jnp.sum(tail, axis=0)
    info = tail[:, 8, :]
    begin = info[:, 0:1] * 16.0 + info[:, 32:33]
    size = info[:, 64:65]
    lane_s = iota((NC, NC * 16), 1)
    owner = (lane_s >> 4) == iota((NC, NC * 16), 0)
    begin_r = jnp.sum(jnp.where(owner, begin, 0.0), axis=0, keepdims=True)
    size_r = jnp.sum(jnp.where(owner, size, 0.0), axis=0, keepdims=True)
    off = iota((1, NC * 16), 1) & 15
    offf = off.astype(F32)
    dest_a = jnp.where(offf < size_r, begin_r + offf, -1.0)
    off_l = offf + 16.0
    dest_l = jnp.where((off < 8) & (off_l < size_r), begin_r + off_l, -1.0)
    off_h = offf + 8.0
    dest_h = jnp.where((off >= 8) & (off_h < size_r), begin_r + off_h, -1.0)
    place = iota((T, NC * 16), 0).astype(F32)
    put_a = onehot(place == dest_a)
    put_l = onehot(place == dest_l)
    put_h = onehot(place == dest_h)

    def routed(c):
        base = 144 + (c // 2) * 16
        return dot(put_a, recv[:, c * 16:(c + 1) * 16, :].reshape(NC * 16, HD)) + dot(
            put_l if c % 2 == 0 else put_h, recv[:, base:base + 16, :].reshape(NC * 16, HD)
        )

    li, lj = iota((HD, HD), 0), iota((HD, HD), 1)
    swap = onehot(li == partner_of(lj)[0])
    qg = qg_ref[...]
    cos, sin = tab[0], tab[1]

    def rotated(x, gain):
        pair = dot(x.astype(BF), swap)
        gain_p = partner_rows(jnp.broadcast_to(gain, (8, HD)))[0:1]
        return rms_factor(x) * (x * (cos * gain) + pair * (sin * gain_p))

    means = []
    for h in range(HL):
        mean = (sums[9 + h:10 + h] + sums[12 + h:13 + h]) * (1.0 / (NC * T))
        means.append(mean)
        mean_p = partner_rows(jnp.broadcast_to(mean, (8, HD)))[0:1]
        k = rotated(routed(3 + h), kg) - (cos * mean + sin * mean_p)
        kv_out[h, 0] = k.astype(BF)
        kv_out[h, 1] = routed(6 + h).astype(BF)
        q_out[h] = rotated(routed(h), qg).astype(BF)

    lax.fori_loop(1, NY, landed(text_y), 0)
    for h in range(HL):
        block = tbuf[:, :, :, h * HD:(h + 1) * HD].astype(F32).reshape(NC, 16, HD)
        k = block[:, :TXD].reshape(TXT, HD)
        t_out[0, h] = (k * rms_factor(k) * kg - means[h]).astype(BF)
        t_out[1, h] = block[:, TXD:].reshape(TXT, HD).astype(BF)

    own_w.wait()
    lax.fori_loop(1, NZ, left(text_z), 0)
    lax.fori_loop(1, NY, left(text_y), 0)
    lax.fori_loop(1, NC, left(piece), 0)
    lax.fori_loop(1, NH, left(weight), 0)
    lax.fori_loop(1, NH, landed(weight), 0)


def attend_kernel(
    q_ref, kv_ref, t_ref, len_ref, wf_ref, b_ref, o_ref,
    win, att, wv, ws, wr, xs, xr, fs, fr, lsem,
):
    me = lax.axis_index("ctx")
    hd = lax.axis_index("head")
    ahead, behind = (me + 1) % NC, (me + NC - 1) % NC
    core = hd % 2
    sib = hd + 1 - 2 * core
    greet([(ahead, hd), (behind, hd), (me, sib)] + [(me, (hd + 2 * e) % NH) for e in (1, 2, 3)])
    load_w = pltpu.make_async_copy(wf_ref, wv, lsem)
    load_w.start()
    met(6)

    def shift(d, h):
        return pltpu.make_async_remote_copy(
            src_ref=kv_ref.at[h] if d == 0 else win.at[d - 1, h], dst_ref=win.at[d, h],
            send_sem=ws.at[d, h], recv_sem=wr.at[d, h],
            device_id=(ahead, hd), device_id_type=MESH,
        )

    def spread(h, e):
        return pltpu.make_async_remote_copy(
            src_ref=att.at[h, hd], dst_ref=att.at[h, hd],
            send_sem=xs.at[h, e], recv_sem=xr.at[h, e],
            device_id=(me, (hd + 2 * e) % NH if e else sib), device_id_type=MESH,
        )

    def hand_on(h, e):
        g = (hd + NH - 2 * e) % NH
        return pltpu.make_async_remote_copy(
            src_ref=att.at[h, g], dst_ref=att.at[h, g],
            send_sem=fs.at[h, e], recv_sem=fr.at[h, e],
            device_id=(me, sib), device_id_type=MESH,
        )

    ones = jnp.ones((T, HD), BF)
    live = iota((TXT, 2 * HD), 0) < len_ref[0]

    def weigh(h, k, v_ext):
        p = jnp.exp2(dot(q_ref[h], k, 1, 1) * SCALE)
        return dot(p.astype(BF), v_ext)

    shift(0, 0).start()
    shift(0, 1).start()

    acc = {}
    for h in range(HL):
        own = weigh(h, kv_ref[h, 0], jnp.concatenate([kv_ref[h, 1], ones], axis=1))
        tv = jnp.concatenate([t_ref[1, h], ones[:TXT]], axis=1)
        tv = jnp.where(live, tv.astype(F32), 0.0).astype(BF)
        acc[h] = own + weigh(h, t_ref[0, h], tv)

    def arrive(d, h):
        shift(d, h).wait_recv()
        if d < WINDOW - 1:
            shift(d + 1, h).start()
        part = weigh(h, win[d, h, 0], jnp.concatenate([win[d, h, 1], ones], axis=1))
        acc[h] = acc[h] + jnp.where(me > d, part, 0.0)

    def finish(h):
        att[h, hd] = (acc[h][:, :HD] / acc[h][:, HD:]).astype(BF)
        for e in (2, 1, 3, 0):
            spread(h, e).start()

    arrive(0, 0)
    arrive(0, 1)
    shift(0, 2).start()
    arrive(1, 0)
    arrive(1, 1)
    arrive(0, 2)
    arrive(2, 0)
    finish(0)
    arrive(2, 1)
    finish(1)
    arrive(1, 2)
    arrive(2, 2)
    finish(2)
    load_w.wait()
    out = jnp.zeros((T, T), F32)
    for h in range(HL):
        for e in (1, 3, 2):
            spread(h, e).wait_recv()
            hand_on(h, e).start()
        spread(h, 0).wait_recv()
        for e in (1, 3, 2):
            hand_on(h, e).wait_recv()
        left = jnp.concatenate([att[h, g] for g in range(NH)], axis=1)
        out = out + dot(left, wv[h])
    o_ref[...] = (out + b_ref[...]).astype(BF)

    for d in range(WINDOW):
        for h in range(HL):
            shift(d, h).wait_send()
    for h in range(HL):
        for e in range(4):
            spread(h, e).wait_send()
        for e in range(1, 4):
            hand_on(h, e).wait_send()


def freq_row():
    row = np.zeros((1, HD), np.float32)
    offset = 0
    for width in (16, 56, 56):
        f = np.float32(256.0) ** (-np.arange(0, width, 2, dtype=np.float32) / np.float32(width))
        row[0, offset:offset + width] = np.concatenate([f, f])
        offset += width
    return row


def on_device(
    qkv_tiles, seq_pos, rope_pos, text_keys, text_values, text_len, q_gain, k_gain, w_out, b_out
):
    vmem = pl.BlockSpec(memory_space=pltpu.VMEM)
    hbm = pl.BlockSpec(memory_space=pl.ANY)
    smem = pl.BlockSpec(memory_space=pltpu.SMEM)
    dma = pltpu.SemaphoreType.DMA
    q, kv, t, wf = pl.pallas_call(
        route_kernel,
        out_shape=(
            jax.ShapeDtypeStruct((HL, T, HD), BF),
            jax.ShapeDtypeStruct((HL, 2, T, HD), BF),
            jax.ShapeDtypeStruct((2, HL, TXT, HD), BF),
            jax.ShapeDtypeStruct((HL, NH * HD, T), BF),
        ),
        in_specs=[vmem] * 8 + [hbm],
        out_specs=(vmem, vmem, vmem, hbm),
        scratch_shapes=[
            pltpu.VMEM((NC, ROWS, HD), BF),
            pltpu.VMEM((NC, ROWS, HD), BF),
            pltpu.VMEM((NY, NZ, 16, T), BF),
            pltpu.VMEM((2, T, HD), F32),
            dma((NC,)), dma((NC,)), dma((NZ,)), dma((NZ,)), dma((NY,)), dma((NY,)),
            dma((NH,)), dma((NH,)), dma,
        ],
        compiler_params=pltpu.CompilerParams(
            collective_id=0, has_side_effects=True, vmem_limit_bytes=48 << 20
        ),
        name="route",
    )(
        qkv_tiles.transpose(1, 0, 2),
        seq_pos.reshape(1, T),
        rope_pos,
        text_keys,
        text_values,
        q_gain.reshape(1, HD),
        k_gain.reshape(1, HD),
        jnp.asarray(freq_row()),
        w_out.reshape(HL, HD, NH * T),
    )
    return pl.pallas_call(
        attend_kernel,
        out_shape=jax.ShapeDtypeStruct((T, T), BF),
        in_specs=[vmem, vmem, vmem, smem, hbm, vmem],
        out_specs=vmem,
        scratch_shapes=[
            pltpu.VMEM((WINDOW, HL, 2, T, HD), BF),
            pltpu.VMEM((HL, NH, T, HD), BF),
            pltpu.VMEM((HL, NH * HD, T), BF),
            dma((WINDOW, HL)), dma((WINDOW, HL)), dma((HL, 4)), dma((HL, 4)),
            dma((HL, 4)), dma((HL, 4)), dma,
        ],
        compiler_params=pltpu.CompilerParams(
            collective_id=1, has_side_effects=True, vmem_limit_bytes=48 << 20
        ),
        name="attend",
    )(q, kv, t, text_len, wf, b_out.reshape(1, T))


def solution(mesh):
    in_specs = (
        P("ctx", None, "head"),
        P("ctx"),
        P(None, "ctx"),
        P("ctx", "head"),
        P("ctx", "head"),
        P(),
        P(),
        P(),
        P("head", None),
        P("head"),
    )
    return jax.shard_map(
        on_device, mesh=mesh, in_specs=in_specs, out_specs=P("ctx", "head"), check_vma=False
    )
```

time: 467 us -> 124 us (0.27); the launches traced: 461 us -> 123 us
  blocking collectives: 161 us -> 0 us
  local copies, waits for them, and re-layouts: 146 us -> 7.29 us
  Pallas kernels: 0 us -> 115 us
  waiting for transfers between devices: 79.4 us -> 0 us
  starting transfers between devices: 29.6 us -> 0 us
  other arithmetic: 20.8 us -> 0 us
  between operations: 14.6 us -> 0.68 us
  matrix products: 9.24 us -> 0 us
    pallas_call x0 -> x2, Pallas kernels: none -> 115 us  [the longest x1 57.8 us: on_device(): pl.pallas_call(route_kernel, out_shape=(jax.ShapeDtypeStruct((HL, T, HD),...]
    scatter x3 -> x0, local copies, waits for them, and re-layouts: 104 us -> none  [the longest x1 59 us: on_device(): routed = jnp.zeros((row_count, 3, span_width), jnp.bfloat16).at[incoming_...]
    all_gather x2 -> x0, blocking collectives: 103 us -> none  [the longest x1 68.1 us: on_device(): lax.all_gather(text_values, 'ctx', axis=0, tiled=True)]
    unnamed x2 -> x0, waiting for transfers between devices: 70.4 us -> none
    psum x1 -> x0, blocking collectives: 57.9 us -> none  [on_device(): key_mean = lax.psum(partial_value, 'ctx') / (row_count * shards)]
    all_to_all x2 -> x0, starting transfers between devices: 21.5 us -> none  [the longest x1 12 us: on_device(): lax.all_to_all(places.reshape(shards, capacity), 'ctx', split_axis=0, con...]
    another operation x6 -> x0, other arithmetic: 9.74 us -> none
    dot_general x11 -> x0, matrix products: 9.24 us -> none  [the longest x5 3.54 us: attend_block(): jnp.einsum('qhd,khd->hqk', query_b, kv_block[0], preferred_element_type=j...]
  transfers between devices with their start and end apart: 6 -> 0, of which waited for: 3 -> 0; matrix products, arithmetic and copies ran while one was open for 15% -> 0% of each run, Pallas kernels for 0% -> 0%
where the time goes in v1:
time: 124 us; the launch traced here: 123 us
  Pallas kernels  115 us (93%)
  local copies, waits for them, and re-layouts  7.29 us (6%)
    pallas_call x1, Pallas kernels, on_device(): pl.pallas_call(route_kernel, out_shape=(jax.ShapeDtypeStruct((HL, T, HD),...  57.8 us
    pallas_call x1, Pallas kernels, on_device(): pl.pallas_call(attend_kernel, out_shape=jax.ShapeDtypeStruct((T, T), BF),...  57.6 us
    unnamed x15, local copies, waits for them, and re-layouts  5.92 us

profile of v1, /device:TPU:1, one launch (start us, length us, event | category | flops | bytes accessed | tf_op | source)
XLA Modules:
  0.0 123.4 jit_solution(4580333903835356501)
XLA Ops:
  0.7 0.7 reshape.15.pos_ref
  1.3 0.7 reshape.19.b_ref
  2.0 0.0 copy-start
  2.0 1.2 copy-done
  3.2 0.0 copy-start.1
  3.2 0.7 copy-done.1
  3.9 0.0 copy-start.2
  3.9 0.7 copy-done.2
  4.6 0.0 copy-start.3
  4.6 0.7 copy-done.3
  5.3 0.0 copy-start.4
  5.3 0.7 copy-done.4
  5.9 0.0 copy-start.5
  5.9 0.7 copy-done.5
  6.6 0.0 copy-start.6
  6.6 0.7 copy-done.6
  7.2 57.8 %route.1 = (bf16[3,384,128]{2,1,0:T(8,128)(2,1)S(1)}, bf16[3,2,384,128]{3,2,1,0:T(8,128)(2,1)S(1)}, bf16[2,3,256,128]{3,2,1,0:T(8,128)(2,1)S(1)}, bf16[3,1024,384]{2,1,0:T(8,128)(2,1)S(1)}) custom-call(bf16[3,384,384]{2,1,0:T(8,128)(2,1)S(1)} %bitcast.4, s32[1,384]{1,0:T(1,128)S(1)} %reshape.15.pos_ref, s32[3,384]{1,0:T(4,128)S(1)} %copy-done.1, ...), custom_call_target="tpu_custom_call" | custom-call | tf_op jit(solution)/shard_map/route/pallas_call | solution.py:386
  65.0 57.6 %attend.1 = bf16[384,384]{1,0:T(8,128)(2,1)S(1)} custom-call(bf16[3,384,128]{2,1,0:T(8,128)(2,1)S(1)} %get-tuple-element.9.q_ref, bf16[3,2,384,128]{3,2,1,0:T(8,128)(2,1)S(1)} %get-tuple-element.10.kv_ref, bf16[2,3,256,128]{3,2,1,0:T(8,128)(2,1)S(1)} %get-tuple-element.11.t_ref, s32[1]{0:T(128)S(6)} %copy.13.len_ref, ...), custom_call_target="tpu_custom_call" | custom-call | tf_op jit(solution)/shard_map/attend/pallas_call | solution.py:419
  122.7 0.7 copy.14
Async XLA Ops:
  2.0 1.2 copy-start
  3.2 0.7 copy-start.1
  3.9 0.7 copy-start.2
  4.6 0.7 copy-start.3
  5.3 0.7 copy-start.4
  5.9 0.7 copy-start.5
  6.6 0.7 copy-start.6

commit v2 on v1

v2 whole, which is shorter than its diff:
```python
import functools

import jax
import jax.numpy as jnp
import numpy as np
from jax import lax
from jax.experimental import pallas as pl
from jax.experimental.pallas import tpu as pltpu
from jax.sharding import PartitionSpec as P

MESH = pl.DeviceIdType.MESH
BF = jnp.bfloat16
F32 = jnp.float32
NC = 32
NY, NZ = 4, 8
NH = 8
T = 384
HL = 3
HD = 128
CUT = 16
KV_ROWS = 160
ROWS = 224
WINDOW = 3
TXT = 256
TXD = 8
GROUP = 8
SCALE = float(np.log2(np.e) / np.sqrt(HD))

OFFSETS = sorted(
    ((dy, dz) for dy in range(NY) for dz in range(NZ) if dy or dz),
    key=lambda o: -(2 * min(o[1], NZ - o[1]) + min(o[0], NY - o[0])),
)


def iota(shape, axis):
    return lax.broadcasted_iota(jnp.int32, shape, axis)


def onehot(mask):
    return jnp.where(mask, 1.0, 0.0).astype(BF)


def dot(a, b, ca=1, cb=0):
    return lax.dot_general(a, b, (((ca,), (cb,)), ((), ())), preferred_element_type=F32)


def partner_of(lane):
    up = (lane < 8) | ((lane >= 16) & (lane < 44)) | ((lane >= 72) & (lane < 100))
    half = jnp.where(lane < 16, 8, 28)
    return jnp.where(up, lane + half, lane - half), up


def partner_row(v):
    v = jnp.broadcast_to(v, (8, HD))
    lane = iota(v.shape, 1)
    _, up = partner_of(lane)
    near = jnp.where(up, pltpu.roll(v, HD - 8, 1), pltpu.roll(v, 8, 1))
    far = jnp.where(up, pltpu.roll(v, HD - 28, 1), pltpu.roll(v, 28, 1))
    return jnp.where(lane < 16, near, far)[0:1]


def rms_factor(x):
    return lax.rsqrt(jnp.mean(x * x, axis=-1, keepdims=True) + 1e-06)


def kernel(
    x_hbm, pos_hbm, rope_hbm, tk_hbm, tv_hbm, len_ref, qg_hbm, kg_hbm, freq_hbm, w_hbm, b_hbm,
    o_ref,
    x, pos_v, rope, rope_far, tk, tv, qg_v, kg_v, freq, bias,
    send, recv, tbuf, tab, puts, acc, qb, kv, text, win, stage, att, wv,
    isem, ssem, rsem, tzs, tzr, tys, tyr, wss, wrs, rs, rr,
    ws, wr, hs, hr, xs, xr, fs, fr,
):
    me = lax.axis_index("ctx")
    hd = lax.axis_index("head")
    my, mz = me // NZ, me % NZ
    core = hd % 2
    sib = hd + 1 - 2 * core

    def home(s):
        z = s % NZ
        return s - z + z + core * (NZ - 1 - 2 * z)

    mirror = my * NZ + NZ - 1 - mz
    shard_me = home(me)
    ahead = home((shard_me + 1) % NC)

    def at(offset):
        return ((my + offset[0]) % NY) * NZ + (mz + offset[1]) % NZ

    barrier = pltpu.get_barrier_semaphore()

    def greet_ctx(d, c):
        pl.semaphore_signal(barrier, inc=1, device_id=((me + d) % NC, hd), device_id_type=MESH)
        return c

    def greet_head(d, c):
        pl.semaphore_signal(barrier, inc=1, device_id=(me, (hd + d) % NH), device_id_type=MESH)
        return c

    fetch = [
        pltpu.make_async_copy(src, dst, isem.at[i])
        for i, (src, dst) in enumerate([
            (pos_hbm, pos_v), (x_hbm.at[1], x.at[1]), (kg_hbm, kg_v), (x_hbm.at[2], x.at[2]),
            (tk_hbm, tk), (tv_hbm, tv), (rope_hbm, rope), (x_hbm.at[0], x.at[0]),
            (freq_hbm, freq), (qg_hbm, qg_v), (b_hbm, bias),
            (
                w_hbm.at[:, :, pl.ds(pl.multiple_of(hd * T, T), T)],
                wv.at[:, pl.ds(pl.multiple_of(hd * HD, HD), HD), :],
            ),
        ])
    ]
    for copy in fetch:
        copy.start()
    lax.fori_loop(1, NC, greet_ctx, 0)
    lax.fori_loop(1, NH, greet_head, 0)

    fetch[0].wait()
    pos = pos_v[...]
    shard = ((pos >> 7) * 171) >> 9
    mine = iota((NC, T), 0) == shard
    first = jnp.min(jnp.where(mine, pos, 1 << 20), axis=1, keepdims=True)
    count = jnp.sum(jnp.where(mine, 1, 0), axis=1, keepdims=True)
    rank = pos - jnp.sum(jnp.where(mine, first, 0), axis=0, keepdims=True)
    code_a = jnp.where(rank < CUT, shard * 16 + rank, -100)
    code_b = jnp.where(rank < CUT, -100, shard * 16 + rank - CUT)
    slot = iota((NC * 16, T), 0)
    pick_a = onehot(slot == code_a)
    pick_b = onehot((slot == code_b) | (slot == code_b + 8))

    fetch[1].wait()
    fetch[2].wait()
    kg = kg_v[...]
    sub16 = iota((16, HD), 0)
    extra = jnp.zeros((16, HD), F32)
    for h in range(HL):
        k = x[1, :, h * HD:(h + 1) * HD].astype(F32)
        total = jnp.sum(k * rms_factor(k), axis=0, keepdims=True) * kg
        high = total.astype(BF).astype(F32)
        extra = jnp.where(sub16 == 9 + h, high, extra)
        extra = jnp.where(sub16 == 12 + h, total - high, extra)
    start = first - iota((NC, 1), 0) * T
    lane = iota((NC, HD), 1)
    meta = jnp.where(lane < 32, start >> 4, jnp.where(lane < 64, start & 15, count)).astype(F32)
    row3 = iota((NC, 16, HD), 1)
    extra = jnp.where(row3 == 8, meta[:, None, :], extra[None])

    def early(comp, h):
        block = x[comp, :, h * HD:(h + 1) * HD]
        return dot(pick_a, block).astype(BF).reshape(NC, 16, HD)

    def late(comp, h):
        return dot(pick_b, x[comp, :, h * HD:(h + 1) * HD]).reshape(NC, 16, HD)

    def both(a, b):
        return jnp.where(row3 < 8, a, b).astype(BF)

    fetch[3].wait()
    fetch[7].wait()
    for c in range(6):
        send[:, c * 16:(c + 1) * 16, :] = early(1 + c // 3, c % 3)
    send[:, 96:112, :] = both(late(1, 0), late(1, 1))
    send[:, 112:128, :] = both(late(1, 2), late(2, 0))
    send[:, 128:144, :] = both(late(2, 1), late(2, 2))
    send[:, 144:160, :] = both(late(0, 2), extra)
    recv[NC - 1, 0:KV_ROWS] = send[shard_me, 0:KV_ROWS]
    fetch[4].wait()
    fetch[5].wait()
    tbuf[my, mz] = jnp.concatenate([tk[...].astype(F32), tv[...].astype(F32)], axis=0).astype(BF)
    fetch[6].wait()

    pl.semaphore_wait(barrier, NC - 1 + NH - 1)

    def text_z(d):
        z = (mz + d) % NZ
        return pltpu.make_async_remote_copy(
            src_ref=tbuf.at[my, mz], dst_ref=tbuf.at[my, mz], send_sem=tzs.at[d], recv_sem=tzr.at[d],
            device_id=(my * NZ + z, hd), device_id_type=MESH,
        )

    def text_y(d):
        y = (my + d) % NY
        return pltpu.make_async_remote_copy(
            src_ref=tbuf.at[my], dst_ref=tbuf.at[my], send_sem=tys.at[d], recv_sem=tyr.at[d],
            device_id=(y * NZ + mz, hd), device_id_type=MESH,
        )

    def piece(i, part):
        to = at(OFFSETS[i])
        rows = pl.ds(0, KV_ROWS) if part == 0 else pl.ds(KV_ROWS, ROWS - KV_ROWS)
        return pltpu.make_async_remote_copy(
            src_ref=send.at[home(to), rows], dst_ref=recv.at[i, rows],
            send_sem=ssem.at[part, i], recv_sem=rsem.at[part, i],
            device_id=(to, hd), device_id_type=MESH,
        )

    def weight(d):
        to = (hd + d) % NH
        return pltpu.make_async_remote_copy(
            src_ref=w_hbm.at[:, :, pl.ds(pl.multiple_of(to * T, T), T)],
            dst_ref=wv.at[:, pl.ds(pl.multiple_of(hd * HD, HD), HD), :],
            send_sem=wss.at[d], recv_sem=wrs.at[d],
            device_id=(me, to), device_id_type=MESH,
        )

    rope_swap = pltpu.make_async_remote_copy(
        src_ref=rope, dst_ref=rope_far, send_sem=rs, recv_sem=rr,
        device_id=(mirror, hd), device_id_type=MESH,
    )

    def shift(d, h):
        return pltpu.make_async_remote_copy(
            src_ref=kv.at[h] if d == 0 else win.at[d - 1, h], dst_ref=win.at[d, h],
            send_sem=ws.at[d, h], recv_sem=wr.at[d, h],
            device_id=(ahead, hd), device_id_type=MESH,
        )

    def go_home(h):
        return pltpu.make_async_remote_copy(
            src_ref=stage.at[h], dst_ref=att.at[h, hd], send_sem=hs.at[h], recv_sem=hr.at[h],
            device_id=(mirror, hd), device_id_type=MESH,
        )

    def spread(h, e):
        return pltpu.make_async_remote_copy(
            src_ref=att.at[h, hd], dst_ref=att.at[h, hd],
            send_sem=xs.at[h, e], recv_sem=xr.at[h, e],
            device_id=(me, (hd + 2 * e) % NH if e else sib), device_id_type=MESH,
        )

    def hand_on(h, e):
        g = (hd + NH - 2 * e) % NH
        return pltpu.make_async_remote_copy(
            src_ref=att.at[h, g], dst_ref=att.at[h, g],
            send_sem=fs.at[h, e], recv_sem=fr.at[h, e],
            device_id=(me, sib), device_id_type=MESH,
        )

    def each(make, n, act):
        def go(d, c):
            getattr(make(d), act)()
            return c
        lax.fori_loop(1, n, go, 0)

    rope_swap.start()
    each(text_z, NZ, "start")
    for i in range(NC - 1):
        piece(i, 0).start()

    for h in range(HL):
        send[:, 160 + h * 16:176 + h * 16, :] = early(0, h)
    send[:, 208:224, :] = both(late(0, 0), late(0, 1))
    recv[NC - 1, KV_ROWS:ROWS] = send[shard_me, KV_ROWS:ROWS]
    for i in range(NC - 1):
        piece(i, 1).start()
    each(weight, NH, "start")

    fetch[8].wait()
    fetch[9].wait()
    rope_swap.wait_recv()
    lane_t = iota((T, HD), 1)
    _, up = partner_of(lane_t)
    eye = iota((T, T), 0) == iota((T, T), 1)
    col = []
    for a in range(3):
        row = jnp.where(core == 1, rope_far[a:a + 1, :], rope[a:a + 1, :]).astype(F32)
        col.append(jnp.sum(jnp.where(eye, row, 0.0), axis=1, keepdims=True))
    angle = jnp.where(lane_t < 16, col[0], jnp.where(lane_t < 72, col[1], col[2])) * freq[...]
    tab[0] = jnp.cos(angle)
    sine = jnp.sin(angle)
    tab[1] = jnp.where(up, -sine, sine)
    li, lj = iota((HD, HD), 0), iota((HD, HD), 1)
    swap = onehot(li == partner_of(lj)[0])

    each(text_z, NZ, "wait_recv")
    each(text_y, NY, "start")

    W = GROUP * 16
    off = iota((1, W), 1) & 15
    offf = off.astype(F32)
    owner = (iota((GROUP, W), 1) >> 4) == iota((GROUP, W), 0)
    place = iota((T, W), 0).astype(F32)
    sums = jnp.zeros((16, HD), F32)

    def rows_of(g, base):
        return recv[g * GROUP:(g + 1) * GROUP, base:base + 16, :].reshape(W, HD)

    def put(g, first_base, last_base, high):
        return dot(puts[g, 0], rows_of(g, first_base)) + dot(
            puts[g, 2 if high else 1], rows_of(g, last_base)
        )

    for g in range(NC // GROUP):
        for i in range(g * GROUP, min((g + 1) * GROUP, NC - 1)):
            piece(i, 0).wait_recv()
        tail = recv[g * GROUP:(g + 1) * GROUP, 144:160, :].astype(F32)
        sums = sums + jnp.sum(tail, axis=0)
        info = tail[:, 8, :]
        begin = jnp.sum(
            jnp.where(owner, info[:, 0:1] * 16.0 + info[:, 32:33], 0.0), axis=0, keepdims=True
        )
        size = jnp.sum(jnp.where(owner, info[:, 64:65], 0.0), axis=0, keepdims=True)
        puts[g, 0] = onehot(place == jnp.where(offf < size, begin + offf, -1.0))
        low = (off < 8) & (offf + 16.0 < size)
        puts[g, 1] = onehot(place == jnp.where(low, begin + offf + 16.0, -1.0))
        high = (off >= 8) & (offf + 8.0 < size)
        puts[g, 2] = onehot(place == jnp.where(high, begin + offf + 8.0, -1.0))
        for c in range(6):
            part = put(g, c * 16, 96 + (c // 2) * 16, c % 2)
            acc[c] = part if g == 0 else acc[c] + part

    cos, sin = tab[0], tab[1]

    def rotated(rows, gain):
        pair = dot(rows.astype(BF), swap)
        return rms_factor(rows) * (rows * (cos * gain) + pair * (sin * partner_row(gain)))

    means = []
    for h in range(HL):
        mean = (sums[9 + h:10 + h] + sums[12 + h:13 + h]) * (1.0 / (NC * T))
        means.append(mean)
        k = rotated(acc[h], kg) - (cos * mean + sin * partner_row(mean))
        kv[h, 0] = k.astype(BF)
        kv[h, 1] = acc[3 + h].astype(BF)
        if h < 2:
            shift(0, h).start()

    each(text_y, NY, "wait_recv")
    for h in range(HL):
        block = tbuf[:, :, :, h * HD:(h + 1) * HD].astype(F32).reshape(NC, 16, HD)
        k = block[:, :TXD].reshape(TXT, HD)
        text[0, h] = (k * rms_factor(k) * kg - means[h]).astype(BF)
        v = jnp.where(iota((TXT, HD), 0) < len_ref[0], block[:, TXD:].reshape(TXT, HD), 0.0)
        text[1, h] = v.astype(BF)

    def forward(d, h):
        shift(d, h).wait_recv()
        if d < WINDOW - 1:
            shift(d + 1, h).start()

    forward(0, 0)
    forward(0, 1)
    shift(0, 2).start()

    qg = qg_v[...]
    for g in range(NC // GROUP):
        for i in range(g * GROUP, min((g + 1) * GROUP, NC - 1)):
            piece(i, 1).wait_recv()
    for h in range(HL):
        rows = None
        for g in range(NC // GROUP):
            part = put(g, 160 + h * 16, 208 if h < 2 else 144, h == 1)
            rows = part if rows is None else rows + part
        qb[h] = rotated(rows, qg).astype(BF)

    ones = jnp.ones((T, HD), BF)
    live = onehot(iota((TXT, HD), 0) < len_ref[0])

    def weigh(h, k, v, beside):
        p = jnp.exp2(dot(qb[h], k, 1, 1) * SCALE)
        return dot(p.astype(BF), jnp.concatenate([v, beside], axis=1))

    num = {}
    for h in range(HL):
        num[h] = weigh(h, kv[h, 0], kv[h, 1], ones) + weigh(h, text[0, h], text[1, h], live)

    def attend(d, h):
        part = weigh(h, win[d, h, 0], win[d, h, 1], ones)
        num[h] = num[h] + jnp.where(shard_me > d, part, 0.0)

    def arrive(d, h):
        forward(d, h)
        attend(d, h)

    def spread_all(h):
        for e in (2, 1, 3, 0):
            spread(h, e).start()

    def finish(h):
        done = (num[h][:, :HD] / num[h][:, HD:]).astype(BF)

        @pl.when(core == 0)
        def _():
            att[h, hd] = done
            spread_all(h)

        @pl.when(core == 1)
        def _():
            stage[h] = done
            go_home(h).start()

    def relay(h):
        @pl.when(core == 1)
        def _():
            go_home(h).wait_recv()
            spread_all(h)

    def hand(h):
        for e in (1, 3, 2):
            spread(h, e).wait_recv()
            hand_on(h, e).start()

    def project(h):
        spread(h, 0).wait_recv()
        for e in (1, 3, 2):
            hand_on(h, e).wait_recv()
        rows = jnp.concatenate([att[h, g] for g in range(NH)], axis=1)
        return dot(rows, wv[h])

    attend(0, 0)
    attend(0, 1)
    arrive(1, 0)
    arrive(1, 1)
    arrive(0, 2)
    arrive(2, 0)
    finish(0)
    arrive(2, 1)
    finish(1)
    relay(0)
    arrive(1, 2)
    arrive(2, 2)
    finish(2)
    relay(1)
    each(weight, NH, "wait_recv")
    fetch[10].wait()
    fetch[11].wait()
    hand(0)
    out = project(0) + bias[...]
    relay(2)
    hand(1)
    out = out + project(1)
    hand(2)
    out = out + project(2)
    o_ref[...] = out.astype(BF)

    rope_swap.wait_send()
    each(text_z, NZ, "wait_send")
    each(text_y, NY, "wait_send")
    each(weight, NH, "wait_send")
    for i in range(NC - 1):
        piece(i, 0).wait_send()
        piece(i, 1).wait_send()
    for h in range(HL):
        for d in range(WINDOW):
            shift(d, h).wait_send()
        for e in range(4):
            spread(h, e).wait_send()
        for e in range(1, 4):
            hand_on(h, e).wait_send()

    @pl.when(core == 1)
    def _():
        for h in range(HL):
            go_home(h).wait_send()


def freq_row():
    row = np.zeros((1, HD), np.float32)
    offset = 0
    for width in (16, 56, 56):
        f = np.float32(256.0) ** (-np.arange(0, width, 2, dtype=np.float32) / np.float32(width))
        row[0, offset:offset + width] = np.concatenate([f, f])
        offset += width
    return row


def on_device(
    qkv_tiles, seq_pos, rope_pos, text_keys, text_values, text_len, q_gain, k_gain, w_out, b_out
):
    hbm = pl.BlockSpec(memory_space=pl.ANY)
    smem = pl.BlockSpec(memory_space=pltpu.SMEM)
    vmem = pltpu.VMEM
    dma = pltpu.SemaphoreType.DMA
    return pl.pallas_call(
        kernel,
        out_shape=jax.ShapeDtypeStruct((T, T), BF),
        in_specs=[hbm] * 5 + [smem] + [hbm] * 5,
        out_specs=pl.BlockSpec(memory_space=pltpu.VMEM),
        scratch_shapes=[
            vmem((3, T, T), BF),
            vmem((1, T), jnp.int32),
            vmem((3, T), jnp.int32),
            vmem((3, T), jnp.int32),
            vmem((TXD, T), BF),
            vmem((TXD, T), BF),
            vmem((1, HD), F32),
            vmem((1, HD), F32),
            vmem((1, HD), F32),
            vmem((1, T), F32),
            vmem((NC, ROWS, HD), BF),
            vmem((NC, ROWS, HD), BF),
            vmem((NY, NZ, 16, T), BF),
            vmem((2, T, HD), F32),
            vmem((NC // GROUP, 3, T, GROUP * 16), BF),
            vmem((6, T, HD), F32),
            vmem((HL, T, HD), BF),
            vmem((HL, 2, T, HD), BF),
            vmem((2, HL, TXT, HD), BF),
            vmem((WINDOW, HL, 2, T, HD), BF),
            vmem((HL, T, HD), BF),
            vmem((HL, NH, T, HD), BF),
            vmem((HL, NH * HD, T), BF),
            dma((12,)),
            dma((2, NC)), dma((2, NC)),
            dma((NZ,)), dma((NZ,)), dma((NY,)), dma((NY,)),
            dma((NH,)), dma((NH,)), dma, dma,
            dma((WINDOW, HL)), dma((WINDOW, HL)), dma((HL,)), dma((HL,)),
            dma((HL, 4)), dma((HL, 4)), dma((HL, 4)), dma((HL, 4)),
        ],
        compiler_params=pltpu.CompilerParams(
            collective_id=0, has_side_effects=True, vmem_limit_bytes=56 << 20
        ),
        name="layer",
    )(
        qkv_tiles.transpose(1, 0, 2),
        seq_pos.reshape(1, T),
        rope_pos,
        text_keys,
        text_values,
        text_len,
        q_gain.reshape(1, HD),
        k_gain.reshape(1, HD),
        jnp.asarray(freq_row()),
        w_out.reshape(HL, HD, NH * T),
        b_out.reshape(1, T),
    )


def solution(mesh):
    in_specs = (
        P("ctx", None, "head"),
        P("ctx"),
        P(None, "ctx"),
        P("ctx", "head"),
        P("ctx", "head"),
        P(),
        P(),
        P(),
        P("head", None),
        P("head"),
    )
    return jax.shard_map(
        on_device, mesh=mesh, in_specs=in_specs, out_specs=P("ctx", "head"), check_vma=False
    )
```

time: 124 us -> 98.7 us (0.80)
  Pallas kernels: 115 us -> 93.6 us
  local copies, waits for them, and re-layouts: 7.29 us -> 4.23 us
    pallas_call x2 -> x1, Pallas kernels: 115 us -> 93.6 us  [on_device(): pl.pallas_call(kernel, out_shape=jax.ShapeDtypeStruct((T, T), BF), in_spe...]
    unnamed x15 -> x1, local copies, waits for them, and re-layouts: 5.92 us -> 1.71 us
where the time goes in v2:
time: 98.7 us; the launch traced here: 98.5 us
  Pallas kernels  93.6 us (95%)
  local copies, waits for them, and re-layouts  4.23 us (4%)
    pallas_call x1, Pallas kernels, on_device(): pl.pallas_call(kernel, out_shape=jax.ShapeDtypeStruct((T, T), BF), in_spe...  93.6 us

profile of v2, /device:TPU:1, one launch (start us, length us, event | category | flops | bytes accessed | tf_op | source)
XLA Modules:
  0.0 98.5 jit_solution(15135063045889253975)
XLA Ops:
  0.7 1.2 %reshape.15.pos_hbm = s32[1,384]{1,0:T(1,128)} reshape(s32[384]{0:T(512)} %param.12) | data formatting | bytes 3072 | tf_op jit(solution)/shard_map/reshape | solution.py:516
  1.9 1.3 %reshape.19.b_hbm = f32[1,384]{1,0:T(1,128)} reshape(f32[384]{0:T(512)} %param.20) | data formatting | bytes 3072 | tf_op jit(solution)/shard_map/reshape | solution.py:525
  3.2 93.6 %layer.1 = bf16[384,384]{1,0:T(8,128)(2,1)} custom-call(bf16[3,384,384]{2,1,0:T(8,128)(2,1)} %bitcast.5, s32[1,384]{1,0:T(1,128)} %reshape.15.pos_hbm, s32[3,384]{1,0:T(4,128)} %rope_hbm.1, bf16[8,384]{1,0:T(8,128)(2,1)} %tk_hbm.1, bf16[8,384]{1,0:T(8,128)(2,1)} %tv_hbm.1, s32[1]{0:T(128)S(6)} %copy.13.len_ref, f32[1,128]{1,0:T(1,128)} %bitcast.6, ...), custom_call_target="tpu_custom_call" | custom-call | tf_op jit(solution)/shard_map/layer/pallas_call | solution.py:474
  96.8 1.7 %copy.14 = bf16[384,384]{1,0:T(8,128)(2,1)} copy(bf16[384,384]{1,0:T(8,128)(2,1)} %layer.1) | data formatting | bytes 589824

commit v3 on v2

--- a/solution.py
+++ b/solution.py
@@ -26,10 +26,8 @@
 GROUP = 8
 SCALE = float(np.log2(np.e) / np.sqrt(HD))
 
-OFFSETS = sorted(
-    ((dy, dz) for dy in range(NY) for dz in range(NZ) if dy or dz),
-    key=lambda o: -(2 * min(o[1], NZ - o[1]) + min(o[0], NY - o[0])),
-)
+FAR = (4, 3, 5, 2, 6, 1, 7, 0)
+OFFSETS = [(dy, dz) for dz in FAR for dy in (3, 2, 1, 0)]
 
 
 def iota(shape, axis):
@@ -116,17 +114,22 @@
     lax.fori_loop(1, NH, greet_head, 0)
 
     fetch[0].wait()
-    pos = pos_v[...]
+    pos = pos_v[...].reshape(1, T)
     shard = ((pos >> 7) * 171) >> 9
-    mine = iota((NC, T), 0) == shard
-    first = jnp.min(jnp.where(mine, pos, 1 << 20), axis=1, keepdims=True)
+    to_z = shard & (NZ - 1)
+    dz = (to_z + core * (NZ - 1 - 2 * to_z) - mz) & (NZ - 1)
+    dy = ((shard >> 3) - my) & (NY - 1)
+    turn = jnp.zeros_like(dz)
+    for place, far in enumerate(FAR):
+        turn = jnp.where(dz == far, place, turn)
+    index = turn * NY + NY - 1 - dy
+    mine = iota((NC, T), 0) == index
+    within = pos - shard * T
+    first = jnp.min(jnp.where(mine, within, T), axis=1, keepdims=True)
     count = jnp.sum(jnp.where(mine, 1, 0), axis=1, keepdims=True)
-    rank = pos - jnp.sum(jnp.where(mine, first, 0), axis=0, keepdims=True)
-    code_a = jnp.where(rank < CUT, shard * 16 + rank, -100)
-    code_b = jnp.where(rank < CUT, -100, shard * 16 + rank - CUT)
-    slot = iota((NC * 16, T), 0)
-    pick_a = onehot(slot == code_a)
-    pick_b = onehot((slot == code_b) | (slot == code_b + 8))
+    rank = within - jnp.sum(jnp.where(mine, first, 0), axis=0, keepdims=True)
+    code_a = jnp.where(rank < CUT, index * 16 + rank, -1)
+    code_b = jnp.where(rank < CUT, -1, index * 8 + rank - CUT)
 
     fetch[1].wait()
     fetch[2].wait()
@@ -139,31 +142,51 @@
         high = total.astype(BF).astype(F32)
         extra = jnp.where(sub16 == 9 + h, high, extra)
         extra = jnp.where(sub16 == 12 + h, total - high, extra)
-    start = first - iota((NC, 1), 0) * T
     lane = iota((NC, HD), 1)
-    meta = jnp.where(lane < 32, start >> 4, jnp.where(lane < 64, start & 15, count)).astype(F32)
-    row3 = iota((NC, 16, HD), 1)
-    extra = jnp.where(row3 == 8, meta[:, None, :], extra[None])
-
-    def early(comp, h):
-        block = x[comp, :, h * HD:(h + 1) * HD]
-        return dot(pick_a, block).astype(BF).reshape(NC, 16, HD)
-
-    def late(comp, h):
-        return dot(pick_b, x[comp, :, h * HD:(h + 1) * HD]).reshape(NC, 16, HD)
+    meta = jnp.where(lane < 32, first >> 4, jnp.where(lane < 64, first & 15, count)).astype(F32)
+    row3 = iota((GROUP, 16, HD), 1)
+
+    def picks(g):
+        a = onehot(iota((GROUP * 16, T), 0) + g * GROUP * 16 == code_a)
+        return a, onehot(iota((GROUP * 8, T), 0) + g * GROUP * 8 == code_b)
+
+    def early(part, c):
+        return part[:, c * HD:(c + 1) * HD].astype(BF).reshape(GROUP, 16, HD)
+
+    def late(part, c):
+        return part[:, c * HD:(c + 1) * HD].reshape(GROUP, 8, HD)
 
     def both(a, b):
-        return jnp.where(row3 < 8, a, b).astype(BF)
+        return jnp.concatenate([a, b], axis=1).astype(BF)
+
+    def pack_kv(g):
+        pick_a, pick_b = picks(g)
+        to = slice(g * GROUP, (g + 1) * GROUP)
+        for comp in (1, 2):
+            part = dot(pick_a, x[comp])
+            for c in range(HL):
+                base = ((comp - 1) * HL + c) * 16
+                send[to, base:base + 16, :] = early(part, c)
+        k, v = dot(pick_b, x[1]), dot(pick_b, x[2])
+        send[to, 96:112, :] = both(late(k, 0), late(k, 1))
+        send[to, 112:128, :] = both(late(k, 2), late(v, 0))
+        send[to, 128:144, :] = both(late(v, 1), late(v, 2))
+        q2 = late(dot(pick_b, x[0, :, 2 * HD:]), 0)
+        info = jnp.where(row3 == 8, meta[to][:, None, :], extra[None])
+        send[to, 144:160, :] = jnp.where(row3 < 8, jnp.concatenate([q2, q2], axis=1), info).astype(BF)
+
+    def pack_q(g):
+        pick_a, pick_b = picks(g)
+        to = slice(g * GROUP, (g + 1) * GROUP)
+        part = dot(pick_a, x[0])
+        for c in range(HL):
+            send[to, 160 + c * 16:176 + c * 16, :] = early(part, c)
+        part = dot(pick_b, x[0, :, :2 * HD])
+        send[to, 208:224, :] = both(late(part, 0), late(part, 1))
 
     fetch[3].wait()
     fetch[7].wait()
-    for c in range(6):
-        send[:, c * 16:(c + 1) * 16, :] = early(1 + c // 3, c % 3)
-    send[:, 96:112, :] = both(late(1, 0), late(1, 1))
-    send[:, 112:128, :] = both(late(1, 2), late(2, 0))
-    send[:, 128:144, :] = both(late(2, 1), late(2, 2))
-    send[:, 144:160, :] = both(late(0, 2), extra)
-    recv[NC - 1, 0:KV_ROWS] = send[shard_me, 0:KV_ROWS]
+    pack_kv(0)
     fetch[4].wait()
     fetch[5].wait()
     tbuf[my, mz] = jnp.concatenate([tk[...].astype(F32), tv[...].astype(F32)], axis=0).astype(BF)
@@ -189,7 +212,7 @@
         to = at(OFFSETS[i])
         rows = pl.ds(0, KV_ROWS) if part == 0 else pl.ds(KV_ROWS, ROWS - KV_ROWS)
         return pltpu.make_async_remote_copy(
-            src_ref=send.at[home(to), rows], dst_ref=recv.at[i, rows],
+            src_ref=send.at[i, rows], dst_ref=recv.at[i, rows],
             send_sem=ssem.at[part, i], recv_sem=rsem.at[part, i],
             device_id=(to, hd), device_id_type=MESH,
         )
@@ -242,17 +265,25 @@
             return c
         lax.fori_loop(1, n, go, 0)
 
+    def pieces(g):
+        return range(g * GROUP, min((g + 1) * GROUP, NC - 1))
+
+    GROUPS = NC // GROUP
+    for i in pieces(0):
+        piece(i, 0).start()
     rope_swap.start()
     each(text_z, NZ, "start")
-    for i in range(NC - 1):
-        piece(i, 0).start()
-
-    for h in range(HL):
-        send[:, 160 + h * 16:176 + h * 16, :] = early(0, h)
-    send[:, 208:224, :] = both(late(0, 0), late(0, 1))
-    recv[NC - 1, KV_ROWS:ROWS] = send[shard_me, KV_ROWS:ROWS]
-    for i in range(NC - 1):
-        piece(i, 1).start()
+    for g in range(1, GROUPS):
+        pack_kv(g)
+        for i in pieces(g):
+            piece(i, 0).start()
+    recv[NC - 1, 0:KV_ROWS] = send[NC - 1, 0:KV_ROWS]
+
+    for g in range(GROUPS):
+        pack_q(g)
+        for i in pieces(g):
+            piece(i, 1).start()
+    recv[NC - 1, KV_ROWS:ROWS] = send[NC - 1, KV_ROWS:ROWS]
     each(weight, NH, "start")
 
     fetch[8].wait()
@@ -285,13 +316,13 @@
     def rows_of(g, base):
         return recv[g * GROUP:(g + 1) * GROUP, base:base + 16, :].reshape(W, HD)
 
-    def put(g, first_base, last_base, high):
-        return dot(puts[g, 0], rows_of(g, first_base)) + dot(
-            puts[g, 2 if high else 1], rows_of(g, last_base)
-        )
-
-    for g in range(NC // GROUP):
-        for i in range(g * GROUP, min((g + 1) * GROUP, NC - 1)):
+    def put(g, blocks, high):
+        rows = [jnp.concatenate([rows_of(g, a), rows_of(g, b)], axis=0) for a, b in blocks]
+        where = jnp.concatenate([puts[g, 0], puts[g, 2 if high else 1]], axis=1)
+        return dot(where, jnp.concatenate(rows, axis=1))
+
+    for g in range(GROUPS):
+        for i in pieces(g):
             piece(i, 0).wait_recv()
         tail = recv[g * GROUP:(g + 1) * GROUP, 144:160, :].astype(F32)
         sums = sums + jnp.sum(tail, axis=0)
@@ -305,9 +336,12 @@
         puts[g, 1] = onehot(place == jnp.where(low, begin + offf + 16.0, -1.0))
         high = (off >= 8) & (offf + 8.0 < size)
         puts[g, 2] = onehot(place == jnp.where(high, begin + offf + 8.0, -1.0))
-        for c in range(6):
-            part = put(g, c * 16, 96 + (c // 2) * 16, c % 2)
-            acc[c] = part if g == 0 else acc[c] + part
+        for odd in range(2):
+            part = put(g, [(c * 16, 96 + (c // 2) * 16) for c in (odd, odd + 2, odd + 4)], odd)
+            acc[odd] = part if g == 0 else acc[odd] + part
+
+    def block(c):
+        return acc[c % 2, :, (c // 2) * HD:(c // 2 + 1) * HD]
 
     cos, sin = tab[0], tab[1]
 
@@ -319,18 +353,18 @@
     for h in range(HL):
         mean = (sums[9 + h:10 + h] + sums[12 + h:13 + h]) * (1.0 / (NC * T))
         means.append(mean)
-        k = rotated(acc[h], kg) - (cos * mean + sin * partner_row(mean))
+        k = rotated(block(h), kg) - (cos * mean + sin * partner_row(mean))
         kv[h, 0] = k.astype(BF)
-        kv[h, 1] = acc[3 + h].astype(BF)
+        kv[h, 1] = block(3 + h).astype(BF)
         if h < 2:
             shift(0, h).start()
 
     each(text_y, NY, "wait_recv")
     for h in range(HL):
-        block = tbuf[:, :, :, h * HD:(h + 1) * HD].astype(F32).reshape(NC, 16, HD)
-        k = block[:, :TXD].reshape(TXT, HD)
+        both_t = tbuf[:, :, :, h * HD:(h + 1) * HD].astype(F32).reshape(NC, 16, HD)
+        k = both_t[:, :TXD].reshape(TXT, HD)
         text[0, h] = (k * rms_factor(k) * kg - means[h]).astype(BF)
-        v = jnp.where(iota((TXT, HD), 0) < len_ref[0], block[:, TXD:].reshape(TXT, HD), 0.0)
+        v = jnp.where(iota((TXT, HD), 0) < len_ref[0], both_t[:, TXD:].reshape(TXT, HD), 0.0)
         text[1, h] = v.astype(BF)
 
     def forward(d, h):
@@ -343,15 +377,15 @@
     shift(0, 2).start()
 
     qg = qg_v[...]
-    for g in range(NC // GROUP):
-        for i in range(g * GROUP, min((g + 1) * GROUP, NC - 1)):
+    rows = [None, None]
+    for g in range(GROUPS):
+        for i in pieces(g):
             piece(i, 1).wait_recv()
+        for odd, blocks in enumerate((((160, 208), (192, 144)), ((176, 208),))):
+            part = put(g, blocks, odd)
+            rows[odd] = part if g == 0 else rows[odd] + part
     for h in range(HL):
-        rows = None
-        for g in range(NC // GROUP):
-            part = put(g, 160 + h * 16, 208 if h < 2 else 144, h == 1)
-            rows = part if rows is None else rows + part
-        qb[h] = rotated(rows, qg).astype(BF)
+        qb[h] = rotated(rows[h % 2][:, (h // 2) * HD:(h // 2 + 1) * HD], qg).astype(BF)
 
     ones = jnp.ones((T, HD), BF)
     live = onehot(iota((TXT, HD), 0) < len_ref[0])
@@ -417,15 +451,22 @@
     arrive(2, 1)
     finish(1)
     relay(0)
+    for i in range(NC - 1):
+        piece(i, 0).wait_send()
+        piece(i, 1).wait_send()
+    rope_swap.wait_send()
+    each(text_z, NZ, "wait_send")
+    each(text_y, NY, "wait_send")
+    each(weight, NH, "wait_send")
+    each(weight, NH, "wait_recv")
+    fetch[10].wait()
+    fetch[11].wait()
     arrive(1, 2)
     arrive(2, 2)
     finish(2)
     relay(1)
-    each(weight, NH, "wait_recv")
-    fetch[10].wait()
-    fetch[11].wait()
     hand(0)
-    out = project(0) + bias[...]
+    out = project(0) + bias[...].reshape(1, T)
     relay(2)
     hand(1)
     out = out + project(1)
@@ -433,13 +474,6 @@
     out = out + project(2)
     o_ref[...] = out.astype(BF)
 
-    rope_swap.wait_send()
-    each(text_z, NZ, "wait_send")
-    each(text_y, NY, "wait_send")
-    each(weight, NH, "wait_send")
-    for i in range(NC - 1):
-        piece(i, 0).wait_send()
-        piece(i, 1).wait_send()
     for h in range(HL):
         for d in range(WINDOW):
             shift(d, h).wait_send()
@@ -478,7 +512,7 @@
         out_specs=pl.BlockSpec(memory_space=pltpu.VMEM),
         scratch_shapes=[
             vmem((3, T, T), BF),
-            vmem((1, T), jnp.int32),
+            vmem((T,), jnp.int32),
             vmem((3, T), jnp.int32),
             vmem((3, T), jnp.int32),
             vmem((TXD, T), BF),
@@ -486,13 +520,13 @@
             vmem((1, HD), F32),
             vmem((1, HD), F32),
             vmem((1, HD), F32),
-            vmem((1, T), F32),
+            vmem((T,), F32),
             vmem((NC, ROWS, HD), BF),
             vmem((NC, ROWS, HD), BF),
             vmem((NY, NZ, 16, T), BF),
             vmem((2, T, HD), F32),
             vmem((NC // GROUP, 3, T, GROUP * 16), BF),
-            vmem((6, T, HD), F32),
+            vmem((2, T, T), F32),
             vmem((HL, T, HD), BF),
             vmem((HL, 2, T, HD), BF),
             vmem((2, HL, TXT, HD), BF),
@@ -513,7 +547,7 @@
         name="layer",
     )(
         qkv_tiles.transpose(1, 0, 2),
-        seq_pos.reshape(1, T),
+        seq_pos,
         rope_pos,
         text_keys,
         text_values,
@@ -522,7 +556,7 @@
         k_gain.reshape(1, HD),
         jnp.asarray(freq_row()),
         w_out.reshape(HL, HD, NH * T),
-        b_out.reshape(1, T),
+        b_out,
     )
 
 

time: 98.7 us -> 96.4 us (0.977)
  local copies, waits for them, and re-layouts: 4.23 us -> 1.71 us
    reshape x2 -> x0, local copies, waits for them, and re-layouts: 2.52 us -> none  [the longest x1 1.28 us: on_device(): b_out.reshape(1, T)]
where the time goes in v3:
time: 96.4 us; the launch traced here: 96.3 us
  Pallas kernels  93.9 us (97%)
  local copies, waits for them, and re-layouts  1.71 us (2%)
    pallas_call x1, Pallas kernels, on_device(): pl.pallas_call(kernel, out_shape=jax.ShapeDtypeStruct((T, T), BF), in_spe...  93.9 us

profile of v3, /device:TPU:1, one launch (start us, length us, event | category | flops | bytes accessed | tf_op | source)
XLA Modules:
  0.0 96.3 jit_solution(8620352173066913914)
XLA Ops:
  0.7 93.9 %layer.1 = bf16[384,384]{1,0:T(8,128)(2,1)} custom-call(bf16[3,384,384]{2,1,0:T(8,128)(2,1)} %bitcast.5, s32[384]{0:T(512)} %pos_hbm.1, s32[3,384]{1,0:T(4,128)} %rope_hbm.1, bf16[8,384]{1,0:T(8,128)(2,1)} %tk_hbm.1, bf16[8,384]{1,0:T(8,128)(2,1)} %tv_hbm.1, s32[1]{0:T(128)S(6)} %copy.13.len_ref, f32[1,128]{1,0:T(1,128)} %bitcast.6, f32[1,128]{1,0:T(1,128)} %bitcast.7, ...), custom_call_target="tpu_custom_call" | custom-call | tf_op jit(solution)/shard_map/layer/pallas_call | solution.py:508
  94.5 1.7 %copy.14 = bf16[384,384]{1,0:T(8,128)(2,1)} copy(bf16[384,384]{1,0:T(8,128)(2,1)} %layer.1) | data formatting | bytes 589824

commit v4 on v3

--- a/solution.py
+++ b/solution.py
@@ -26,8 +26,18 @@
 GROUP = 8
 SCALE = float(np.log2(np.e) / np.sqrt(HD))
 
-FAR = (4, 3, 5, 2, 6, 1, 7, 0)
-OFFSETS = [(dy, dz) for dz in FAR for dy in (3, 2, 1, 0)]
+DY = (2, 1, 3, 0)
+DZ = (3, 5, 4, 0, 1, 7, 2, 6)
+OFFSETS = [(dy, dz) for dy in DY for dz in DZ]
+OWN = OFFSETS.index((0, 0))
+
+UNITS = ((0, 0, T), (1, 0, T), (2, 0, T // 2), (2, T // 2, T // 2))
+
+STEPS = (
+    "f00", "f01", "f02", "Q", "o0", "f10", "o1", "f11", "o2", "f12", "a00", "a01", "a02", "a10", "a11", "a12",
+    "f20", "a20", "F0", "f21", "a21", "F1", "R0", "W", "f22", "a22", "F2", "a23", "F3", "R1", "H0", "R2",
+    "R3", "H1", "H2", "H3", "P0", "P1", "P2", "P3",
+)
 
 
 def iota(shape, axis):
@@ -119,10 +129,11 @@
     to_z = shard & (NZ - 1)
     dz = (to_z + core * (NZ - 1 - 2 * to_z) - mz) & (NZ - 1)
     dy = ((shard >> 3) - my) & (NY - 1)
-    turn = jnp.zeros_like(dz)
-    for place, far in enumerate(FAR):
-        turn = jnp.where(dz == far, place, turn)
-    index = turn * NY + NY - 1 - dy
+    index = jnp.zeros_like(dz)
+    for place, d in enumerate(DZ):
+        index = jnp.where(dz == d, place, index)
+    for place, d in enumerate(DY):
+        index = jnp.where(dy == d, index + place * NZ, index)
     mine = iota((NC, T), 0) == index
     within = pos - shard * T
     first = jnp.min(jnp.where(mine, within, T), axis=1, keepdims=True)
@@ -238,24 +249,29 @@
             device_id=(ahead, hd), device_id_type=MESH,
         )
 
-    def go_home(h):
-        return pltpu.make_async_remote_copy(
-            src_ref=stage.at[h], dst_ref=att.at[h, hd], send_sem=hs.at[h], recv_sem=hr.at[h],
+    def slab(u, g):
+        h, r, n = UNITS[u]
+        return att.at[h, g, pl.ds(r, n)]
+
+    def go_home(u):
+        h, r, n = UNITS[u]
+        return pltpu.make_async_remote_copy(
+            src_ref=stage.at[h, pl.ds(r, n)], dst_ref=slab(u, hd), send_sem=hs.at[u], recv_sem=hr.at[u],
             device_id=(mirror, hd), device_id_type=MESH,
         )
 
-    def spread(h, e):
-        return pltpu.make_async_remote_copy(
-            src_ref=att.at[h, hd], dst_ref=att.at[h, hd],
-            send_sem=xs.at[h, e], recv_sem=xr.at[h, e],
+    def spread(u, e):
+        return pltpu.make_async_remote_copy(
+            src_ref=slab(u, hd), dst_ref=slab(u, hd),
+            send_sem=xs.at[u, e], recv_sem=xr.at[u, e],
             device_id=(me, (hd + 2 * e) % NH if e else sib), device_id_type=MESH,
         )
 
-    def hand_on(h, e):
+    def hand_on(u, e):
         g = (hd + NH - 2 * e) % NH
         return pltpu.make_async_remote_copy(
-            src_ref=att.at[h, g], dst_ref=att.at[h, g],
-            send_sem=fs.at[h, e], recv_sem=fr.at[h, e],
+            src_ref=slab(u, g), dst_ref=slab(u, g),
+            send_sem=fs.at[u, e], recv_sem=fr.at[u, e],
             device_id=(me, sib), device_id_type=MESH,
         )
 
@@ -266,7 +282,7 @@
         lax.fori_loop(1, n, go, 0)
 
     def pieces(g):
-        return range(g * GROUP, min((g + 1) * GROUP, NC - 1))
+        return [i for i in range(g * GROUP, (g + 1) * GROUP) if i != OWN]
 
     GROUPS = NC // GROUP
     for i in pieces(0):
@@ -277,13 +293,13 @@
         pack_kv(g)
         for i in pieces(g):
             piece(i, 0).start()
-    recv[NC - 1, 0:KV_ROWS] = send[NC - 1, 0:KV_ROWS]
+    recv[OWN, 0:KV_ROWS] = send[OWN, 0:KV_ROWS]
 
     for g in range(GROUPS):
         pack_q(g)
         for i in pieces(g):
             piece(i, 1).start()
-    recv[NC - 1, KV_ROWS:ROWS] = send[NC - 1, KV_ROWS:ROWS]
+    recv[OWN, KV_ROWS:ROWS] = send[OWN, KV_ROWS:ROWS]
     each(weight, NH, "start")
 
     fetch[8].wait()
@@ -356,8 +372,7 @@
         k = rotated(block(h), kg) - (cos * mean + sin * partner_row(mean))
         kv[h, 0] = k.astype(BF)
         kv[h, 1] = block(3 + h).astype(BF)
-        if h < 2:
-            shift(0, h).start()
+        shift(0, h).start()
 
     each(text_y, NY, "wait_recv")
     for h in range(HL):
@@ -372,120 +387,130 @@
         if d < WINDOW - 1:
             shift(d + 1, h).start()
 
-    forward(0, 0)
-    forward(0, 1)
-    shift(0, 2).start()
-
-    qg = qg_v[...]
-    rows = [None, None]
-    for g in range(GROUPS):
-        for i in pieces(g):
-            piece(i, 1).wait_recv()
-        for odd, blocks in enumerate((((160, 208), (192, 144)), ((176, 208),))):
-            part = put(g, blocks, odd)
-            rows[odd] = part if g == 0 else rows[odd] + part
-    for h in range(HL):
-        qb[h] = rotated(rows[h % 2][:, (h // 2) * HD:(h // 2 + 1) * HD], qg).astype(BF)
+    def queries():
+        qg = qg_v[...]
+        rows = [None, None]
+        for g in range(GROUPS):
+            for i in pieces(g):
+                piece(i, 1).wait_recv()
+            for odd, blocks in enumerate((((160, 208), (192, 144)), ((176, 208),))):
+                part = put(g, blocks, odd)
+                rows[odd] = part if g == 0 else rows[odd] + part
+        for h in range(HL):
+            qb[h] = rotated(rows[h % 2][:, (h // 2) * HD:(h // 2 + 1) * HD], qg).astype(BF)
 
     ones = jnp.ones((T, HD), BF)
     live = onehot(iota((TXT, HD), 0) < len_ref[0])
 
-    def weigh(h, k, v, beside):
-        p = jnp.exp2(dot(qb[h], k, 1, 1) * SCALE)
+    def weigh(q, k, v, beside):
+        p = jnp.exp2(dot(q, k, 1, 1) * SCALE)
         return dot(p.astype(BF), jnp.concatenate([v, beside], axis=1))
 
     num = {}
-    for h in range(HL):
-        num[h] = weigh(h, kv[h, 0], kv[h, 1], ones) + weigh(h, text[0, h], text[1, h], live)
-
-    def attend(d, h):
-        part = weigh(h, win[d, h, 0], win[d, h, 1], ones)
-        num[h] = num[h] + jnp.where(shard_me > d, part, 0.0)
-
-    def arrive(d, h):
-        forward(d, h)
-        attend(d, h)
-
-    def spread_all(h):
-        for e in (2, 1, 3, 0):
-            spread(h, e).start()
-
-    def finish(h):
-        done = (num[h][:, :HD] / num[h][:, HD:]).astype(BF)
+
+    def own(h):
+        q = qb[h]
+        num[h] = weigh(q, kv[h, 0], kv[h, 1], ones) + weigh(q, text[0, h], text[1, h], live)
+
+    def attend(d, h, r=0, n=T):
+        part = weigh(qb[h, r:r + n], win[d, h, 0], win[d, h, 1], ones)
+        return num[h][r:r + n] + jnp.where(shard_me > d, part, 0.0)
+
+    def finish(u, total):
+        h, r, n = UNITS[u]
+        done = (total[:, :HD] / total[:, HD:]).astype(BF)
 
         @pl.when(core == 0)
         def _():
-            att[h, hd] = done
-            spread_all(h)
+            att[h, hd, r:r + n] = done
+            spread_all(u)
 
         @pl.when(core == 1)
         def _():
-            stage[h] = done
-            go_home(h).start()
-
-    def relay(h):
+            stage[h, r:r + n] = done
+            go_home(u).start()
+
+    def spread_all(u):
+        for e in (2, 1, 3, 0):
+            spread(u, e).start()
+
+    def relay(u):
         @pl.when(core == 1)
         def _():
-            go_home(h).wait_recv()
-            spread_all(h)
-
-    def hand(h):
+            go_home(u).wait_recv()
+            spread_all(u)
+
+    def hand(u):
         for e in (1, 3, 2):
-            spread(h, e).wait_recv()
-            hand_on(h, e).start()
-
-    def project(h):
-        spread(h, 0).wait_recv()
+            spread(u, e).wait_recv()
+            hand_on(u, e).start()
+
+    def project(u):
+        h, r, n = UNITS[u]
+        spread(u, 0).wait_recv()
         for e in (1, 3, 2):
-            hand_on(h, e).wait_recv()
-        rows = jnp.concatenate([att[h, g] for g in range(NH)], axis=1)
+            hand_on(u, e).wait_recv()
+        rows = jnp.concatenate([att[h, g, r:r + n] for g in range(NH)], axis=1)
         return dot(rows, wv[h])
 
-    attend(0, 0)
-    attend(0, 1)
-    arrive(1, 0)
-    arrive(1, 1)
-    arrive(0, 2)
-    arrive(2, 0)
-    finish(0)
-    arrive(2, 1)
-    finish(1)
-    relay(0)
-    for i in range(NC - 1):
-        piece(i, 0).wait_send()
-        piece(i, 1).wait_send()
-    rope_swap.wait_send()
-    each(text_z, NZ, "wait_send")
-    each(text_y, NY, "wait_send")
-    each(weight, NH, "wait_send")
-    each(weight, NH, "wait_recv")
-    fetch[10].wait()
-    fetch[11].wait()
-    arrive(1, 2)
-    arrive(2, 2)
-    finish(2)
-    relay(1)
-    hand(0)
-    out = project(0) + bias[...].reshape(1, T)
-    relay(2)
-    hand(1)
-    out = out + project(1)
-    hand(2)
-    out = out + project(2)
-    o_ref[...] = out.astype(BF)
+    def settle():
+        for g in range(GROUPS):
+            for i in pieces(g):
+                piece(i, 0).wait_send()
+                piece(i, 1).wait_send()
+        rope_swap.wait_send()
+        each(text_z, NZ, "wait_send")
+        each(text_y, NY, "wait_send")
+        each(weight, NH, "wait_send")
+        each(weight, NH, "wait_recv")
+        fetch[10].wait()
+        fetch[11].wait()
+
+    out = None
+    last = {}
+    for step in STEPS:
+        kind, arg = step[0], [int(c) for c in step[1:]]
+        if kind == "f":
+            forward(*arg)
+        elif kind == "Q":
+            queries()
+        elif kind == "o":
+            own(*arg)
+        elif kind == "a" and arg[0] < WINDOW - 1:
+            num[arg[1]] = attend(*arg)
+        elif kind == "a":
+            last[arg[1]] = attend(arg[0], *UNITS[arg[1]])
+        elif kind == "F":
+            finish(arg[0], last[arg[0]])
+        elif kind == "R":
+            relay(*arg)
+        elif kind == "W":
+            settle()
+        elif kind == "H":
+            hand(*arg)
+        elif kind == "P":
+            h, r, n = UNITS[arg[0]]
+            part = project(*arg)
+            if h == 0:
+                out = part + bias[...].reshape(1, T)
+            elif h == 1:
+                out = out + part
+            else:
+                o_ref[r:r + n] = (out[r:r + n] + part).astype(BF)
 
     for h in range(HL):
         for d in range(WINDOW):
             shift(d, h).wait_send()
+    for u in range(len(UNITS)):
         for e in range(4):
-            spread(h, e).wait_send()
+            spread(u, e).wait_send()
         for e in range(1, 4):
-            hand_on(h, e).wait_send()
+            hand_on(u, e).wait_send()
 
     @pl.when(core == 1)
     def _():
-        for h in range(HL):
-            go_home(h).wait_send()
+        for u in range(len(UNITS)):
+            go_home(u).wait_send()
 
 
 def freq_row():
@@ -538,8 +563,8 @@
             dma((2, NC)), dma((2, NC)),
             dma((NZ,)), dma((NZ,)), dma((NY,)), dma((NY,)),
             dma((NH,)), dma((NH,)), dma, dma,
-            dma((WINDOW, HL)), dma((WINDOW, HL)), dma((HL,)), dma((HL,)),
-            dma((HL, 4)), dma((HL, 4)), dma((HL, 4)), dma((HL, 4)),
+            dma((WINDOW, HL)), dma((WINDOW, HL)), dma((4,)), dma((4,)),
+            dma((4, 4)), dma((4, 4)), dma((4, 4)), dma((4, 4)),
         ],
         compiler_params=pltpu.CompilerParams(
             collective_id=0, has_side_effects=True, vmem_limit_bytes=56 << 20

time: 96.4 us -> 95.7 us (level)
  no operation moved by 1% of the time
where the time goes in v4:
time: 95.7 us; the launch traced here: 95.6 us
  Pallas kernels  93.2 us (97%)
  local copies, waits for them, and re-layouts  1.71 us (2%)
    pallas_call x1, Pallas kernels, on_device(): pl.pallas_call(kernel, out_shape=jax.ShapeDtypeStruct((T, T), BF), in_spe...  93.2 us

profile of v4, /device:TPU:1, one launch (start us, length us, event | category | flops | bytes accessed | tf_op | source)
XLA Modules:
  0.0 95.6 jit_solution(12915237022152362651)
XLA Ops:
  0.7 93.2 %layer.1 = bf16[384,384]{1,0:T(8,128)(2,1)} custom-call(bf16[3,384,384]{2,1,0:T(8,128)(2,1)} %bitcast.5, s32[384]{0:T(512)} %pos_hbm.1, s32[3,384]{1,0:T(4,128)} %rope_hbm.1, bf16[8,384]{1,0:T(8,128)(2,1)} %tk_hbm.1, bf16[8,384]{1,0:T(8,128)(2,1)} %tv_hbm.1, s32[1]{0:T(128)S(6)} %copy.13.len_ref, f32[1,128]{1,0:T(1,128)} %bitcast.6, f32[1,128]{1,0:T(1,128)} %bitcast.7, ...), custom_call_target="tpu_custom_call" | custom-call | tf_op jit(solution)/shard_map/layer/pallas_call | solution.py:533
  93.9 1.7 %copy.14 = bf16[384,384]{1,0:T(8,128)(2,1)} copy(bf16[384,384]{1,0:T(8,128)(2,1)} %layer.1) | data formatting | bytes 589824

commit v5 on v4

--- a/solution.py
+++ b/solution.py
@@ -36,7 +36,7 @@
 STEPS = (
     "f00", "f01", "f02", "Q", "o0", "f10", "o1", "f11", "o2", "f12", "a00", "a01", "a02", "a10", "a11", "a12",
     "f20", "a20", "F0", "f21", "a21", "F1", "R0", "W", "f22", "a22", "F2", "a23", "F3", "R1", "H0", "R2",
-    "R3", "H1", "H2", "H3", "P0", "P1", "P2", "P3",
+    "R3", "H1", "Z", "H2", "H3", "P0", "P1", "P2", "P3",
 )
 
 
@@ -466,12 +466,28 @@
         fetch[10].wait()
         fetch[11].wait()
 
+    def left(u):
+        for e in range(4):
+            spread(u, e).wait_send()
+        for e in range(1, 4):
+            hand_on(u, e).wait_send()
+
+        @pl.when(core == 1)
+        def _():
+            go_home(u).wait_send()
+
     out = None
     last = {}
     for step in STEPS:
         kind, arg = step[0], [int(c) for c in step[1:]]
         if kind == "f":
             forward(*arg)
+        elif kind == "Z":
+            for h in range(HL):
+                for d in range(WINDOW):
+                    shift(d, h).wait_send()
+            left(0)
+            left(1)
         elif kind == "Q":
             queries()
         elif kind == "o":
@@ -498,19 +514,8 @@
             else:
                 o_ref[r:r + n] = (out[r:r + n] + part).astype(BF)
 
-    for h in range(HL):
-        for d in range(WINDOW):
-            shift(d, h).wait_send()
-    for u in range(len(UNITS)):
-        for e in range(4):
-            spread(u, e).wait_send()
-        for e in range(1, 4):
-            hand_on(u, e).wait_send()
-
-    @pl.when(core == 1)
-    def _():
-        for u in range(len(UNITS)):
-            go_home(u).wait_send()
+    left(2)
+    left(3)
 
 
 def freq_row():

time: 95.7 us -> 95.7 us (level)
  no operation moved by 1% of the time
where the time goes in v5:
time: 95.7 us; the launch traced here: 95.5 us
  Pallas kernels  93.2 us (97%)
  local copies, waits for them, and re-layouts  1.71 us (2%)
    pallas_call x1, Pallas kernels, on_device(): pl.pallas_call(kernel, out_shape=jax.ShapeDtypeStruct((T, T), BF), in_spe...  93.2 us

profile of v5, /device:TPU:1, one launch (start us, length us, event | category | flops | bytes accessed | tf_op | source)
XLA Modules:
  0.0 95.5 jit_solution(14450305695015045071)
XLA Ops:
  0.7 93.2 %layer.1 = bf16[384,384]{1,0:T(8,128)(2,1)} custom-call(bf16[3,384,384]{2,1,0:T(8,128)(2,1)} %bitcast.5, s32[384]{0:T(512)} %pos_hbm.1, s32[3,384]{1,0:T(4,128)} %rope_hbm.1, bf16[8,384]{1,0:T(8,128)(2,1)} %tk_hbm.1, bf16[8,384]{1,0:T(8,128)(2,1)} %tv_hbm.1, s32[1]{0:T(128)S(6)} %copy.13.len_ref, f32[1,128]{1,0:T(1,128)} %bitcast.6, f32[1,128]{1,0:T(1,128)} %bitcast.7, ...), custom_call_target="tpu_custom_call" | custom-call | tf_op jit(solution)/shard_map/layer/pallas_call | solution.py:538
  93.8 1.7 %copy.14 = bf16[384,384]{1,0:T(8,128)(2,1)} copy(bf16[384,384]{1,0:T(8,128)(2,1)} %layer.1) | data formatting | bytes 589824
